TPU v7x, 32 devices: a whole 2x2x4 slice. The times are simulated.
32 devices in a mesh: shard: 4 (over z), ctx: 4 (over y, x), tp: 2 (over core).
Axes of the slice: x: 2, y: 2, z: 4, core: 2. Of those that a mesh axis runs over, the one named last changes fastest.
Arguments:
- layer_entry_input: bfloat16 [2048, 1024], P(('shard', 'ctx')), may hold values from -6 to 6
- first_layer_values: bfloat16 [2048, 1024], P(('shard', 'ctx'), 'tp'), may hold values from -6 to 6
- segments: int32 [2048], P(('shard', 'ctx')), may hold values from 0 to 2, as said below
- cotangent: bfloat16 [2048, 1024], P(('shard', 'ctx')), may hold values from -6 to 6
- layernorm_gain: bfloat16 [2, 1024], P(None, 'shard'), may hold values from 0.5 to 1.5
- layernorm_bias: bfloat16 [2, 1024], P(None, 'shard'), may hold values from -1.75 to 1.75
- token_shift_coefs: bfloat16 [7, 1024], P(None, 'shard'), may hold values from 0 to 1
- channel_coefficients: bfloat16 [8, 16, 64], P(None, 'tp', 'shard'), may hold values from -10 to 4
- receptance_key_value_weight: bfloat16 [3, 1024, 1024], P(None, 'shard', 'tp'), may hold values from -0.1875 to 0.1875
- output_weight: bfloat16 [1024, 1024], P('tp', 'shard'), may hold values from -0.375 to 0.375
- low_rank_down: bfloat16 [1024, 288], P('shard'), may hold values from -0.1875 to 0.1875
- low_rank_upper: bfloat16 [288, 1024], P('shard', 'tp'), may hold values from -0.75 to 0.75
- channel_key_weight: bfloat16 [1024, 4096], P('shard', 'tp'), may hold values from -0.1875 to 0.1875
- channel_value_weight: bfloat16 [4096, 1024], P('tp', 'shard'), may hold values from -0.09375 to 0.09375
Outputs:
- layer_output: bfloat16 [2048, 1024], P(('shard', 'ctx'))
- grad_x: float32 [2048, 1024], P(('shard', 'ctx'))
- grad_value_first: float32 [2048, 1024], P(('shard', 'ctx'), 'tp')
- grad_norm_gain: float32 [2, 1024], P(None, 'shard')
- grad_norm_bias: float32 [2, 1024], P(None, 'shard')
- grad_mix_coef: float32 [6, 1024], P(None, 'shard')
- grad_decay_mix: float32 [1024], P('shard')
- grad_head_coef: float32 [8, 16, 64], P(None, 'tp', 'shard')
- grad_w_rkv: float32 [3, 1024, 1024], P(None, 'shard', 'tp')
- grad_w_out: float32 [1024, 1024], P('tp', 'shard')
- grad_lora_down: float32 [1024, 288], P('shard')
- grad_lora_up: float32 [288, 1024], P('shard', 'tp')
- grad_w_ffn_in: float32 [1024, 4096], P('shard', 'tp')
- grad_w_ffn_out: float32 [4096, 1024], P('tp', 'shard')
Inputs may be any that keep to these rules, and one draw needn't show every extreme that they name: `segments`: each sequence holds exactly three documents numbered 0, 1, 2 in order; document 1 starts within the first 128 tokens of the sequence and ends within its last 128 tokens.
All inputs are finite; a program needn't handle non-finite values.
Results may differ from a plain program's by a relative error of at most 0.025.
The roundings to bfloat16 on the way count: a program that leaves them out, or rounds other values in their place, can miss the bound.
Values may be sent and summed in bfloat16 or wider, within the bound.
A program may use at most 128 MiB of HBM per device.

v0:
```python
import jax
import jax.numpy as jnp
from jax import lax
from jax.sharding import PartitionSpec as P

DECAY_LOW_RANK = 64
RATE_RANK = 64
VALUE_RANK = 32


highest = lax.Precision.HIGHEST
steps_per_block = 16


def passed_along(block, axis, distance):
    devices = range(lax.axis_size(axis))
    route = [(i - distance, i) for i in devices if i - distance in devices]
    return lax.ppermute(block, axis, route)


def entering(part, axis, combine, identity):
    place = lax.axis_index(axis)
    gathered = jax.tree.map(lambda a: lax.all_gather(a, axis), part)
    state = jax.tree.map(lambda a, e: jnp.zeros_like(a) + jnp.asarray(e, a.dtype), part, identity)

    def one(hop, state):
        return combine(
            state, jax.tree.map(lambda a: lax.dynamic_index_in_dim(a, hop, 0, False), gathered)
        )

    return lax.fori_loop(0, place, one, state)


def carried_in(array, axis, combine, identity):
    peers, place = (lax.axis_size(axis), lax.axis_index(axis))
    everything = jax.tree.map(
        lambda part, kind: lax.all_gather(part.astype(kind), axis),
        array,
        jax.tree.map(lambda a: jnp.bfloat16 if a.dtype == jnp.float32 else a.dtype, array),
    )
    start = jax.tree.map(
        lambda part, zero: jnp.broadcast_to(jnp.asarray(zero, part.dtype), part.shape),
        array,
        identity,
    )

    def hop(k, before):
        at = peers - 1 - k
        reached = at > place
        new = combine(
            before, jax.tree.map(lambda part, own: part[at].astype(own.dtype), everything, array)
        )
        return jax.tree.map(lambda a, b: jnp.where(reached, a, b), new, before)

    return lax.fori_loop(0, peers, hop, start)


def matrix_product(left, right):
    return jnp.dot(left, right, preferred_element_type=jnp.float32)


def inner_product(left, right):
    return lax.dot_general(
        left, right, (((0,), (0,)), ((), ())), preferred_element_type=jnp.float32
    )


def across_heads(left, right):
    return lax.dot_general(
        left, right, (((1,), (1,)), ((), ())), preferred_element_type=jnp.float32
    )


def layer_norm(values, gain, bias):
    mean = jnp.mean(values, -1, keepdims=True)
    centred = values - mean
    spread = jnp.mean(centred * centred, -1, keepdims=True)
    return centred * lax.rsqrt(spread + 1e-05) * gain + bias


def token_mix(standardized_vectors, prev_row, keep, blend_amounts):
    shifted = jnp.concatenate([prev_row, standardized_vectors[:-1]], 0) * keep[:, None]
    delta = shifted - standardized_vectors
    return standardized_vectors[None] + delta[None] * blend_amounts[:, None, :]


def head_leading(
    receptance_before,
    key_before_norm,
    value_before_mix,
    decay_low_rank,
    rate_low_rank,
    value_low_rank,
    first_layer_values,
    blend_amounts,
):
    count = receptance_before.shape[0]
    heads = blend_amounts.shape[1]

    def split_parts(item_entry):
        return item_entry.reshape(count, heads, -1)

    decay_logarithm = -jax.nn.softplus(-(blend_amounts[0] + split_parts(decay_low_rank))) - 0.5
    decay_factor = jnp.exp(-jnp.exp(decay_logarithm))
    rate_values = jax.nn.sigmoid(blend_amounts[1] + split_parts(rate_low_rank))
    lookup_projected_vectors = split_parts(key_before_norm)
    content_projected_vectors = split_parts(value_before_mix)
    content_projected_vectors = content_projected_vectors + (
        split_parts(first_layer_values) - content_projected_vectors
    ) * jax.nn.sigmoid(blend_amounts[2] + split_parts(value_low_rank))
    removal = lookup_projected_vectors * blend_amounts[3]
    removal = removal * lax.rsqrt(jnp.sum(removal * removal, -1, keepdims=True) + 1e-06)
    lookup_projected_vectors = lookup_projected_vectors * (
        1.0 + (rate_values - 1.0) * blend_amounts[4]
    )
    return (
        split_parts(receptance_before),
        decay_factor,
        lookup_projected_vectors,
        content_projected_vectors,
        -removal,
        removal * rate_values,
    )


def block_step(state, inputs):
    r_blk, d_blk, k_blk, v_blk, a_blk, b_blk, m_blk = inputs
    length = m_blk.shape[0]
    log_w = jnp.log(d_blk)
    total_g = jnp.cumsum(log_w, 0)
    before_g = total_g - log_w
    resets = jnp.cumsum(1.0 - m_blk)
    same = (resets[:, None] == resets[None, :]).astype(jnp.float32)
    first_entry = (resets == 0.0).astype(jnp.float32)
    row_ids = jnp.arange(length)[:, None]
    col_ids = jnp.arange(length)[None, :]
    mask_before = (col_ids < row_ids).astype(jnp.float32) * same
    mask_after = (col_ids <= row_ids).astype(jnp.float32) * same
    grow_before = jnp.exp(before_g)
    grow_total = jnp.exp(total_g)
    shrink_total = jnp.exp(-total_g)
    a_scaled = a_blk * grow_before
    r_scaled = r_blk * grow_total
    b_scaled = b_blk * shrink_total
    k_scaled = k_blk * shrink_total
    l_pull = jnp.einsum("shk,jhk->hsj", a_scaled, b_scaled, precision=highest) * mask_before[None]
    l_key = jnp.einsum("shk,jhk->hsj", a_scaled, k_scaled, precision=highest) * mask_before[None]
    start_pull = (
        jnp.einsum("hrk,shk->hsr", state, a_scaled, precision=highest) * first_entry[None, :, None]
    )
    rhs = start_pull + jnp.einsum("hsj,jhr->hsr", l_key, v_blk, precision=highest)
    unit = jnp.broadcast_to(jnp.eye(length, dtype=jnp.float32), l_pull.shape)
    solver = unit + l_pull
    power = l_pull
    for level in range(max((length - 1).bit_length() - 1, 0)):
        power = jnp.einsum("hij,hjk->hik", power, power, precision=highest)
        solver = jnp.einsum("hij,hjk->hik", solver, unit + power, precision=highest)
    pulled = jnp.einsum("hsj,hjr->hsr", solver, rhs, precision=highest)
    start_raw = (
        jnp.einsum("hrk,thk->htr", state, r_scaled, precision=highest) * first_entry[None, :, None]
    )
    q_pull = jnp.einsum("thk,shk->hts", r_scaled, b_scaled, precision=highest) * mask_after[None]
    q_key = jnp.einsum("thk,shk->hts", r_scaled, k_scaled, precision=highest) * mask_after[None]
    raw_output = (
        start_raw
        + jnp.einsum("hts,hsr->htr", q_pull, pulled, precision=highest)
        + jnp.einsum("hts,shr->htr", q_key, v_blk, precision=highest)
    )
    last_g = total_g[-1]
    tail = jnp.exp(last_g[None] - total_g) * same[-1][:, None, None]
    new_state = (
        first_entry[-1] * state * jnp.exp(last_g)[:, None, :]
        + jnp.einsum("hsr,shk->hrk", pulled, b_blk * tail, precision=highest)
        + jnp.einsum("shr,shk->hrk", v_blk, k_blk * tail, precision=highest)
    )
    return (new_state, jnp.swapaxes(raw_output, 0, 1))


def run_local(
    acceptance_vectors,
    decay_factor,
    lookup_projected_vectors,
    content_projected_vectors,
    removal_direction,
    insert_direction,
    keep,
):
    count, heads, width = acceptance_vectors.shape
    blocks = count // steps_per_block
    values = jnp.concatenate(
        [jnp.zeros((count, heads, width), jnp.float32), content_projected_vectors], -1
    )
    identity = jnp.broadcast_to(jnp.eye(width, dtype=jnp.float32), (heads, width, width))
    start = jnp.concatenate([identity, jnp.zeros((heads, width, width), jnp.float32)], 1)
    inputs = tuple(
        (
            item_entry.reshape((blocks, steps_per_block) + item_entry.shape[1:])
            for item_entry in (
                acceptance_vectors,
                decay_factor,
                lookup_projected_vectors,
                values,
                removal_direction,
                insert_direction,
                keep,
            )
        )
    )
    final, outputs = lax.scan(jax.checkpoint(block_step), start, inputs)
    return (outputs.reshape((count, heads, 2 * width)), final)


def head_trailing(
    raw_output,
    acceptance_vectors,
    lookup_projected_vectors,
    content_projected_vectors,
    gate,
    blend_amounts,
):
    mean = jnp.mean(raw_output, -1, keepdims=True)
    centred = raw_output - mean
    spread = jnp.mean(centred * centred, -1, keepdims=True)
    standardized_vectors = (
        centred * lax.rsqrt(spread + 0.00064) * blend_amounts[6] + blend_amounts[7]
    )
    current_step_extra = (
        jnp.sum(acceptance_vectors * lookup_projected_vectors * blend_amounts[5], -1, keepdims=True)
        * content_projected_vectors
    )
    combined_result = standardized_vectors + current_step_extra
    return combined_result.reshape(gate.shape) * gate


def compose(earlier, later):
    return (
        jnp.einsum("hij,hjk->hik", earlier[0], later[0], precision=highest),
        jnp.einsum("hij,hjk->hik", earlier[1], later[0], precision=highest) + later[1],
    )


def to_owners(members):
    return (
        lax.psum_scatter(
            members[0].astype(jnp.bfloat16), "shard", scatter_dimension=1, tiled=True
        ).astype(jnp.float32),
        lax.psum_scatter(
            members[1].astype(jnp.bfloat16), "shard", scatter_dimension=2, tiled=True
        ).astype(jnp.float32),
        lax.psum_scatter(
            members[2].astype(jnp.bfloat16), "shard", scatter_dimension=1, tiled=True
        ).astype(jnp.float32),
        lax.psum_scatter(
            members[3].astype(jnp.bfloat16), "shard", scatter_dimension=1, tiled=True
        ).astype(jnp.float32),
        lax.psum_scatter(
            members[4].astype(jnp.bfloat16), "shard", scatter_dimension=0, tiled=True
        ).astype(jnp.float32),
        lax.psum_scatter(
            members[5].astype(jnp.bfloat16), "shard", scatter_dimension=0, tiled=True
        ).astype(jnp.float32),
        lax.psum_scatter(
            members[6].astype(jnp.bfloat16), "shard", scatter_dimension=0, tiled=True
        ).astype(jnp.float32),
        lax.psum_scatter(
            members[7].astype(jnp.bfloat16), "shard", scatter_dimension=1, tiled=True
        ).astype(jnp.float32),
    )


def over_blocks(members):
    return (
        lax.psum_scatter(
            members[0].astype(jnp.bfloat16), "ctx", scatter_dimension=2, tiled=True
        ).astype(jnp.float32),
        lax.psum_scatter(
            members[1].astype(jnp.bfloat16), "ctx", scatter_dimension=0, tiled=True
        ).astype(jnp.float32),
        lax.psum_scatter(
            members[2].astype(jnp.bfloat16), "ctx", scatter_dimension=2, tiled=True
        ).astype(jnp.float32),
        lax.psum_scatter(
            members[3].astype(jnp.bfloat16), "ctx", scatter_dimension=0, tiled=True
        ).astype(jnp.float32),
        lax.psum_scatter(
            members[4].astype(jnp.bfloat16), "ctx", scatter_dimension=1, tiled=True
        ).astype(jnp.float32),
        lax.psum_scatter(
            members[5].astype(jnp.bfloat16), "ctx", scatter_dimension=1, tiled=True
        ).astype(jnp.float32),
        lax.psum_scatter(
            members[6].astype(jnp.bfloat16), "ctx", scatter_dimension=1, tiled=True
        ).astype(jnp.float32),
        lax.psum_scatter(
            members[7].astype(jnp.bfloat16), "ctx", scatter_dimension=0, tiled=True
        ).astype(jnp.float32),
    )


def per_device(
    layer_entry_input,
    first_layer_values,
    segments,
    cotangent,
    layernorm_gain,
    layernorm_bias,
    token_shift_coefs,
    channel_coefficients,
    receptance_key_value_weight,
    output_weight,
    low_rank_down,
    low_rank_upper,
    channel_key_weight,
    channel_value_weight,
):
    gains, biases, mixes, blend_amounts, proj, out_proj, down, upper_factor, ffn_in, ffn_out = (
        lax.all_gather(layernorm_gain, "shard", axis=1, tiled=True),
        lax.all_gather(layernorm_bias, "shard", axis=1, tiled=True),
        lax.all_gather(token_shift_coefs, "shard", axis=1, tiled=True),
        lax.all_gather(channel_coefficients, "shard", axis=2, tiled=True),
        lax.all_gather(receptance_key_value_weight, "shard", axis=1, tiled=True),
        lax.all_gather(output_weight, "shard", axis=1, tiled=True),
        lax.all_gather(low_rank_down, "shard", axis=0, tiled=True),
        lax.all_gather(low_rank_upper, "shard", axis=0, tiled=True),
        lax.all_gather(channel_key_weight, "shard", axis=0, tiled=True),
        lax.all_gather(channel_value_weight, "shard", axis=1, tiled=True),
    )
    gains = gains.astype(jnp.float32)
    biases = biases.astype(jnp.float32)
    mixes = mixes.astype(jnp.float32)
    blend_amounts = blend_amounts.astype(jnp.float32)
    boundary_first = DECAY_LOW_RANK
    boundary_second = boundary_first + RATE_RANK
    boundary_third = boundary_second + VALUE_RANK
    inputs_f = layer_entry_input.astype(jnp.float32)
    seg_next = (segments + 1).astype(jnp.float32)
    standardized_vectors, norm1_back = jax.vjp(layer_norm, inputs_f, gains[0], biases[0])
    prev_row, prev_seg = passed_along((standardized_vectors[-1:], seg_next[-1:]), "ctx", 1)
    keep = jnp.concatenate(
        [
            (prev_seg == seg_next[:1]).astype(jnp.float32),
            (segments[1:] == segments[:-1]).astype(jnp.float32),
        ]
    )

    def mix_local(normed_in, prev_in, coef_in):
        return token_mix(normed_in, prev_in, keep, coef_in)

    mix_all, mix1_back = jax.vjp(mix_local, standardized_vectors, prev_row, mixes[:6])
    mixed = mix_all.astype(jnp.bfloat16)
    receptance_before = matrix_product(mixed[0], proj[0])
    key_before_norm = matrix_product(mixed[2], proj[1])
    value_before_mix = matrix_product(mixed[3], proj[2])
    decay_inner_rows = jnp.tanh(matrix_product(mixed[1], down[:, :boundary_first]))
    rate_inner_rows = matrix_product(mixed[4], down[:, boundary_first:boundary_second])
    value_inner_rows = matrix_product(mixed[3], down[:, boundary_second:boundary_third])
    gate_inner_rows = jax.nn.sigmoid(matrix_product(mixed[5], down[:, boundary_third:]))
    hidden_bfloat = [
        item_entry.astype(jnp.bfloat16)
        for item_entry in (decay_inner_rows, rate_inner_rows, value_inner_rows, gate_inner_rows)
    ]
    upper_factor_parts = [
        upper_factor[:boundary_first],
        upper_factor[boundary_first:boundary_second],
        upper_factor[boundary_second:boundary_third],
        upper_factor[boundary_third:],
    ]
    low_rank_maps = [
        matrix_product(hidden_bfloat[index_value], upper_factor_parts[index_value])
        for index_value in range(4)
    ]
    fronts, front_back = jax.vjp(
        head_leading,
        receptance_before,
        key_before_norm,
        value_before_mix,
        low_rank_maps[0],
        low_rank_maps[1],
        low_rank_maps[2],
        first_layer_values.astype(jnp.float32),
        blend_amounts,
    )
    (
        acceptance_vectors,
        decay_factor,
        lookup_projected_vectors,
        content_projected_vectors,
        removal_direction,
        insert_direction,
    ) = fronts
    heads = blend_amounts.shape[1]
    width = blend_amounts.shape[2]
    identity = jnp.broadcast_to(jnp.eye(width, dtype=jnp.float32), (heads, width, width))
    empty_state = jnp.zeros((heads, width, width), jnp.float32)

    def chain_local(r_in, d_in, k_in, v_in, a_in, b_in):
        return run_local(r_in, d_in, k_in, v_in, a_in, b_in, keep)

    (raw_both, final_both), chain_back = jax.vjp(
        chain_local,
        acceptance_vectors,
        decay_factor,
        lookup_projected_vectors,
        content_projected_vectors,
        removal_direction,
        insert_direction,
    )
    transfer = final_both[:, :width]
    offset = final_both[:, width:]
    raw_trans = raw_both[..., :width]
    raw_off = raw_both[..., width:]
    incoming = entering((transfer, offset), "ctx", compose, (identity, empty_state))[1]
    raw_output = raw_off + jnp.einsum("hvi,thi->thv", incoming, raw_trans, precision=highest)
    combined_result, trailing_backward = jax.vjp(
        head_trailing,
        raw_output,
        acceptance_vectors,
        lookup_projected_vectors,
        content_projected_vectors,
        low_rank_maps[3],
        blend_amounts,
    )
    merged_bf = combined_result.astype(jnp.bfloat16)
    attn = lax.psum(matrix_product(merged_bf, out_proj).astype(jnp.bfloat16), "tp").astype(
        jnp.float32
    )
    mid = inputs_f + attn
    normed2, norm2_back = jax.vjp(layer_norm, mid, gains[1], biases[1])
    prev2 = passed_along(normed2[-1:], "ctx", 1)
    mix2, mix2_back = jax.vjp(mix_local, normed2, prev2, mixes[6:])
    mix2_bf = mix2[0].astype(jnp.bfloat16)
    pre2 = matrix_product(mix2_bf, ffn_in)
    active = jax.nn.relu(pre2)
    hidden2_bf = (active * active).astype(jnp.bfloat16)
    ffn = lax.psum(matrix_product(hidden2_bf, ffn_out).astype(jnp.bfloat16), "tp").astype(
        jnp.float32
    )
    result = (mid + ffn).astype(jnp.bfloat16)
    g_ffn_out = inner_product(hidden2_bf, cotangent)
    d_pre2 = (across_heads(cotangent, ffn_out) * 2.0 * active).astype(jnp.bfloat16)
    g_ffn_in = inner_product(mix2_bf, d_pre2)
    d_mix2 = lax.psum(across_heads(d_pre2, ffn_in).astype(jnp.bfloat16), "tp").astype(jnp.float32)
    d_normed2, d_prev2, d_coef2 = mix2_back(d_mix2[None])
    d_row2 = passed_along(d_prev2, "ctx", -1)
    d_normed2 = d_normed2.at[-1:].add(d_row2)
    d_mid_norm, d_gain2, d_bias2 = norm2_back(d_normed2)
    d_mid = cotangent.astype(jnp.float32) + d_mid_norm
    d_attn_bf = d_mid.astype(jnp.bfloat16)
    g_out = inner_product(merged_bf, d_attn_bf)
    d_merged = across_heads(d_attn_bf, out_proj)
    d_raw, d_recept_post, d_keyed_post, d_valued_post, d_gate, d_coef_post = trailing_backward(
        d_merged
    )
    local_in = jnp.einsum("thv,thi->hvi", d_raw, raw_trans, precision=highest)
    flipped = jnp.swapaxes(transfer, 1, 2)
    d_outgoing = carried_in((flipped, local_in), "ctx", compose, (identity, empty_state))[1]
    d_raw_both = jnp.concatenate(
        [jnp.einsum("hvi,thv->thi", incoming, d_raw, precision=highest), d_raw], -1
    )
    d_final_both = jnp.concatenate(
        [jnp.einsum("hvi,hvj->hij", incoming, d_outgoing, precision=highest), d_outgoing], 1
    )
    chain_grads = chain_back((d_raw_both, d_final_both))
    front_grads = front_back(
        (
            d_recept_post + chain_grads[0],
            chain_grads[1],
            d_keyed_post + chain_grads[2],
            d_valued_post + chain_grads[3],
            chain_grads[4],
            chain_grads[5],
        )
    )
    d_rp_bf = front_grads[0].astype(jnp.bfloat16)
    d_kp_bf = front_grads[1].astype(jnp.bfloat16)
    d_vp_bf = front_grads[2].astype(jnp.bfloat16)
    low_rank_gradients = [
        front_grads[3].astype(jnp.bfloat16),
        front_grads[4].astype(jnp.bfloat16),
        front_grads[5].astype(jnp.bfloat16),
        d_gate.astype(jnp.bfloat16),
    ]
    d_first = front_grads[6]
    g_head = front_grads[7] + d_coef_post
    g_proj = jnp.stack(
        [
            inner_product(mixed[0], d_rp_bf),
            inner_product(mixed[2], d_kp_bf),
            inner_product(mixed[3], d_vp_bf),
        ]
    )
    gate_up_weight = jnp.concatenate(
        [
            inner_product(hidden_bfloat[index_value], low_rank_gradients[index_value])
            for index_value in range(4)
        ],
        0,
    )
    d_hidden_part = jnp.concatenate(
        [
            across_heads(low_rank_gradients[index_value], upper_factor_parts[index_value])
            for index_value in range(4)
        ],
        1,
    )
    d_xr, d_xk, d_xv, d_hidden = (
        lax.psum(across_heads(d_rp_bf, proj[0]).astype(jnp.bfloat16), "tp").astype(jnp.float32),
        lax.psum(across_heads(d_kp_bf, proj[1]).astype(jnp.bfloat16), "tp").astype(jnp.float32),
        lax.psum(across_heads(d_vp_bf, proj[2]).astype(jnp.bfloat16), "tp").astype(jnp.float32),
        lax.psum(d_hidden_part.astype(jnp.bfloat16), "tp").astype(jnp.float32),
    )
    d_pre_decay = (
        d_hidden[:, :boundary_first] * (1.0 - decay_inner_rows * decay_inner_rows)
    ).astype(jnp.bfloat16)
    d_pre_rate = d_hidden[:, boundary_first:boundary_second].astype(jnp.bfloat16)
    d_pre_value = d_hidden[:, boundary_second:boundary_third].astype(jnp.bfloat16)
    d_pre_gate = (d_hidden[:, boundary_third:] * gate_inner_rows * (1.0 - gate_inner_rows)).astype(
        jnp.bfloat16
    )
    g_down = jnp.concatenate(
        [
            inner_product(mixed[1], d_pre_decay),
            inner_product(mixed[4], d_pre_rate),
            inner_product(mixed[3], d_pre_value),
            inner_product(mixed[5], d_pre_gate),
        ],
        1,
    )
    d_mixes = jnp.stack(
        [
            d_xr,
            across_heads(d_pre_decay, down[:, :boundary_first]),
            d_xk,
            d_xv + across_heads(d_pre_value, down[:, boundary_second:boundary_third]),
            across_heads(d_pre_rate, down[:, boundary_first:boundary_second]),
            across_heads(d_pre_gate, down[:, boundary_third:]),
        ]
    )
    d_normed, d_prev, d_coef1 = mix1_back(d_mixes)
    d_row = passed_along(d_prev, "ctx", -1)
    d_normed = d_normed.at[-1:].add(d_row)
    d_input_norm, d_gain1, d_bias1 = norm1_back(d_normed)
    d_input = d_mid + d_input_norm
    owners = lax.axis_size("shard")
    row_grads = jnp.concatenate(
        [jnp.stack([d_gain1, d_gain2]), jnp.stack([d_bias1, d_bias2]), d_coef1, d_coef2], 0
    )
    row_grads = row_grads.reshape(row_grads.shape[0], owners, -1)
    members = (row_grads, g_head, g_proj, g_out, g_down, gate_up_weight, g_ffn_in, g_ffn_out)
    summed = over_blocks(to_owners(members))
    grads = (
        lax.all_gather(summed[0].astype(jnp.bfloat16), "ctx", axis=2, tiled=True).astype(
            jnp.float32
        ),
        lax.all_gather(summed[1].astype(jnp.bfloat16), "ctx", axis=0, tiled=True).astype(
            jnp.float32
        ),
        lax.all_gather(summed[2].astype(jnp.bfloat16), "ctx", axis=2, tiled=True).astype(
            jnp.float32
        ),
        lax.all_gather(summed[3].astype(jnp.bfloat16), "ctx", axis=0, tiled=True).astype(
            jnp.float32
        ),
        lax.all_gather(summed[4].astype(jnp.bfloat16), "ctx", axis=1, tiled=True).astype(
            jnp.float32
        ),
        lax.all_gather(summed[5].astype(jnp.bfloat16), "ctx", axis=1, tiled=True).astype(
            jnp.float32
        ),
        lax.all_gather(summed[6].astype(jnp.bfloat16), "ctx", axis=1, tiled=True).astype(
            jnp.float32
        ),
        lax.all_gather(summed[7].astype(jnp.bfloat16), "ctx", axis=0, tiled=True).astype(
            jnp.float32
        ),
    )
    row_sums = grads[0].reshape(grads[0].shape[0], -1)
    mix_rows = jnp.concatenate([row_sums[4:5], row_sums[6:11]], 0)
    return (
        result,
        d_input,
        d_first,
        row_sums[0:2],
        row_sums[2:4],
        mix_rows,
        row_sums[5],
        grads[1],
        grads[2],
        grads[3],
        grads[4],
        grads[5],
        grads[6],
        grads[7],
    )


def solution(mesh):
    return jax.shard_map(
        per_device,
        mesh=mesh,
        in_specs=(
            P(("shard", "ctx"), None),
            P(("shard", "ctx"), "tp"),
            P(("shard", "ctx")),
            P(("shard", "ctx"), None),
            P(None, "shard"),
            P(None, "shard"),
            P(None, "shard"),
            P(None, "tp", "shard"),
            P(None, "shard", "tp"),
            P("tp", "shard"),
            P("shard", None),
            P("shard", "tp"),
            P("shard", "tp"),
            P("tp", "shard"),
        ),
        out_specs=(
            P(("shard", "ctx"), None),
            P(("shard", "ctx"), None),
            P(("shard", "ctx"), "tp"),
            P(None, "shard"),
            P(None, "shard"),
            P(None, "shard"),
            P("shard"),
            P(None, "tp", "shard"),
            P(None, "shard", "tp"),
            P("tp", "shard"),
            P("shard", None),
            P("shard", "tp"),
            P("shard", "tp"),
            P("tp", "shard"),
        ),
        check_vma=False,
    )
```

profile of v0, /device:TPU:0, one launch (start us, length us, event | category | flops | bytes accessed | tf_op | source)
XLA Modules:
  0.0 1373.8 jit_solution(8770667461584655964)
XLA Ops:
  8.0 12.8 all_gather.80
  43.2 14.4 %all_gather.78 = bf16[8,8,64]{1,0,2:T(8,128)(2,1)S(1)} all-gather(bf16[8,8,16]{1,0,2:T(8,128)(2,1)S(1)} %copy.559), channel_id=1, replica_groups=mesh['shard'=4,'ctx'=4,'tp'=2] {'shard'}, dimensions={2}, use_global_device_ids=true | all-gather | bytes 10240 | tf_op jit(solution)/shard_map/all_gather | solution.py:320
  58.5 13.2 all_gather.81
  71.8 19.7 %all_gather.82 = bf16[1024,288]{0,1:T(8,128)(2,1)} all-gather(bf16[256,288]{0,1:T(8,128)(2,1)S(1)} %copy-done.64), channel_id=1, replica_groups=mesh['shard'=4,'ctx'=4,'tp'=2] {'shard'}, dimensions={0}, use_global_device_ids=true | all-gather | bytes 737280 | tf_op jit(solution)/shard_map/all_gather | solution.py:323
  91.5 15.6 %all_gather.83 = bf16[288,512]{1,0:T(8,128)(2,1)S(1)} all-gather(bf16[72,512]{1,0:T(8,128)(2,1)S(1)} %copy-done.66), channel_id=1, replica_groups=mesh['shard'=4,'ctx'=4,'tp'=2] {'shard'}, dimensions={0}, use_global_device_ids=true | all-gather | bytes 368640 | tf_op jit(solution)/shard_map/all_gather | solution.py:324
  138.6 73.7 %while.74 = (s32[]{:T(128)}, f32[8,128,64]{1,2,0:T(8,128)S(1)}, f32[8,16,8,128]{3,2,1,0:T(8,128)S(1)}, f32[8,8,128,64]{2,3,1,0:T(8,128)}, f32[8,16]{1,0:T(8,128)...) while((s32[]{:T(128)}, f32[8,128,64]{1,2,0:T(8,128)S(1)}, ...), condition=%wide.region_6.7_spmd.clone.clone, body=%wide.region_3.6_spmd.clone.clone.sunk | while | flops 72132912 | bytes 4454873 | solution.py:209
  212.6 13.6 all-gather
  226.2 11.7 all-gather.1
  248.7 19.2 %all-reduce.20.cloned.1.call-done = bf16[128,1024]{1,0:T(8,128)(2,1)} async-done(((bf16[128,1024]{1,0:T(8,128)(2,1)}), bf16[128,1024]{1,0:T(8,128)(2,1)}) %all-reduce.20.cloned.1.call-update) | async-done | bytes 262160 | tf_op jit(solution)/shard_map/psum | solution.py:424
  274.9 10.6 all-gather.2
  286.5 64.9 %all-gather.15.cloned.1.call-done = bf16[1024,2048]{1,0:T(8,128)(2,1)} async-done(((bf16[256,2048]{1,0:T(8,128)(2,1)}), bf16[1024,2048]{1,0:T(8,128)(2,1)}) %all-gather.15.cloned.1.call-update) | async-done | bytes 4194320 | tf_op jit(solution)/shard_map/all_gather | solution.py:325
  354.4 77.6 %all-gather.17.cloned.1.call-done = bf16[2048,1024]{1,0:T(8,128)(2,1)} async-done(((bf16[2048,256]{1,0:T(8,128)(2,1)}), bf16[2048,1024]{1,0:T(8,128)(2,1)}) %all-gather.17.cloned.1.call-update) | async-done | bytes 4194320 | tf_op jit(solution)/shard_map/all_gather | solution.py:326
  442.6 12.9 all-reduce.22.cloned.1.call-done
  475.5 12.0 all-gather.3
  504.8 215.2 %while.73 = (s32[]{:T(128)}, f32[8,128,64]{1,2,0:T(8,128)S(1)}, f32[8,16,8,64]{3,2,1,0:T(8,128)}, f32[8,16,8,64]{3,2,1,0:T(8,128)}, f32[8,16,8,64]{3,2,1,0:T(8,1...) while((s32[]{:T(128)}, f32[8,128,64]{1,2,0:T(8,128)S(1)}, ...), condition=%wide.region_30.31_spmd, body=%wide.region_24.30_spmd.sunk | while | flops 172069680 | bytes 11185197 | solution.py:209
  807.9 45.3 %reduce-scatter.38.cloned.1.call-done = bf16[256,2048]{1,0:T(8,128)(2,1)} async-done(((bf16[1024,2048]{1,0:T(8,128)(2,1)}), bf16[256,2048]{1,0:T(8,128)(2,1)}) %reduce-scatter.38.cloned.1.call-update) | async-done | bytes 1048592 | tf_op jit(solution)/shard_map/reduce_scatter | solution.py:262
  853.3 79.6 %reduce-scatter.42.cloned.1.call-done = bf16[2048,256]{1,0:T(8,128)(2,1)} async-done(((bf16[2048,1024]{1,0:T(8,128)(2,1)}), bf16[2048,256]{1,0:T(8,128)(2,1)}) %reduce-scatter.42.cloned.1.call-update) | async-done | bytes 1048592 | tf_op jit(solution)/shard_map/reduce_scatter | solution.py:265
  935.3 20.8 %reduce-scatter.36.cloned.1.call-done = bf16[72,512]{1,0:T(8,128)(2,1)} async-done(((bf16[288,512]{1,0:T(8,128)(2,1)}), bf16[72,512]{1,0:T(8,128)(2,1)}) %reduce-scatter.36.cloned.1.call-update) | async-done | bytes 73744 | tf_op jit(solution)/shard_map/reduce_scatter | solution.py:259
  957.8 18.3 %reduce-scatter.26.cloned.1.call-done = bf16[11,1,256]{2,0,1:T(8,128)(2,1)} async-done(((bf16[11,4,256]{2,0,1:T(8,128)(2,1)}), bf16[11,1,256]{2,0,1:T(8,128)(2,1)}) %reduce-scatter.26.cloned.1.call-update) | async-done | bytes 5648 | tf_op jit(solution)/shard_map/reduce_scatter | solution.py:244
  977.6 21.5 %reduce-scatter.34.cloned.1.call-done = bf16[256,288]{0,1:T(8,128)(2,1)} async-done(((bf16[1024,288]{0,1:T(8,128)(2,1)}), bf16[256,288]{0,1:T(8,128)(2,1)}) %reduce-scatter.34.cloned.1.call-update) | async-done | bytes 147472 | tf_op jit(solution)/shard_map/reduce_scatter | solution.py:256
  999.1 28.4 %reduce-scatter.30.cloned.1.call-done = bf16[512,256]{1,0:T(8,128)(2,1)} async-done(((bf16[512,1024]{1,0:T(8,128)(2,1)}), bf16[512,256]{1,0:T(8,128)(2,1)}) %reduce-scatter.30.cloned.1.call-update) | async-done | bytes 262160 | tf_op jit(solution)/shard_map/reduce_scatter | solution.py:253
  1027.7 61.0 %reduce-scatter.28.cloned.1.call-done = bf16[3,256,512]{2,1,0:T(8,128)(2,1)} async-done(((bf16[3,1024,512]{2,1,0:T(8,128)(2,1)}), bf16[3,256,512]{2,1,0:T(8,128)(2,1)}) %reduce-scatter.28.cloned.1.call-update) | async-done | bytes 786448 | tf_op jit(solution)/shard_map/reduce_scatter | solution.py:250
  1091.4 27.8 %reduce-scatter.40.cloned.1.call-done = bf16[256,512]{1,0:T(8,128)(2,1)} async-done(((bf16[256,2048]{1,0:T(8,128)(2,1)}), bf16[256,512]{1,0:T(8,128)(2,1)}) %reduce-scatter.40.cloned.1.call-update) | async-done | bytes 262160 | tf_op jit(solution)/shard_map/reduce_scatter | solution.py:291
  1119.3 30.7 %reduce-scatter.44.cloned.1.call-done = bf16[512,256]{1,0:T(8,128)(2,1)} async-done(((bf16[2048,256]{1,0:T(8,128)(2,1)}), bf16[512,256]{1,0:T(8,128)(2,1)}) %reduce-scatter.44.cloned.1.call-update) | async-done | bytes 262160 | tf_op jit(solution)/shard_map/reduce_scatter | solution.py:294
  1152.1 19.4 %reduce-scatter.48.cloned.1.call-done = bf16[16,64]{1,0:T(8,128)(2,1)} async-done(((bf16[64,64]{1,0:T(8,128)(2,1)}), bf16[16,64]{1,0:T(8,128)(2,1)}) %reduce-scatter.48.cloned.1.call-update) | async-done | bytes 2064
  1172.4 16.0 %all-reduce.13 = bf16[8,8,16]{2,1,0:T(8,128)(2,1)S(1)} all-reduce(bf16[8,8,16]{2,1,0:T(8,128)(2,1)S(1)} %copy.657), channel_id=9, replica_groups=mesh['shard'=4,'ctx'=4,'tp'=2] {'ctx'}, use_global_device_ids=true, to_apply=%region_56.57.clone | all-reduce | flops 1024 | bytes 4096
  1207.8 16.1 %reduce-scatter.46.cloned.1.call-done = bf16[64,11]{1,0:T(8,128)(2,1)} async-done(((bf16[256,11]{1,0:T(8,128)(2,1)}), bf16[64,11]{1,0:T(8,128)(2,1)}) %reduce-scatter.46.cloned.1.call-update) | async-done | bytes 1424
  1259.4 17.8 %reduce-scatter.32.cloned.1.call-done = bf16[128,256]{1,0:T(8,128)(2,1)} async-done(((bf16[512,256]{1,0:T(8,128)(2,1)}), bf16[128,256]{1,0:T(8,128)(2,1)}) %reduce-scatter.32.cloned.1.call-update) | async-done | bytes 65552 | tf_op jit(solution)/shard_map/reduce_scatter | solution.py:282
  1287.0 19.8 %reduce-scatter.50.cloned.1.call-done = bf16[128,768]{1,0:T(8,128)(2,1)} async-done(((bf16[512,768]{1,0:T(8,128)(2,1)}), bf16[128,768]{1,0:T(8,128)(2,1)}) %reduce-scatter.50.cloned.1.call-update) | async-done | bytes 196624
  1308.1 11.8 all_gather.98
  1321.2 14.2 %all-gather.19.cloned.1.call-done = bf16[256,2048]{1,0:T(8,128)(2,1)} async-done(((bf16[256,512]{1,0:T(8,128)(2,1)}), bf16[256,2048]{1,0:T(8,128)(2,1)}) %all-gather.19.cloned.1.call-update) | async-done | bytes 1048592 | tf_op jit(solution)/shard_map/all_gather | solution.py:570
  1338.2 25.6 %all-gather.21.cloned.1.call-done = bf16[2048,256]{1,0:T(8,128)(2,1)} async-done(((bf16[512,256]{1,0:T(8,128)(2,1)}), bf16[2048,256]{1,0:T(8,128)(2,1)}) %all-gather.21.cloned.1.call-update) | async-done | bytes 1048592 | tf_op jit(solution)/shard_map/all_gather | solution.py:573
  (1488 shorter events, 586.6 us)
Async XLA Ops:
  7.2 111.1 %all-gather.11.cloned.1.call-start = ((), (), s32[]{:S(2)}) async-start(), calls=%async_computation.15 | async-start | bytes 3932160 | tf_op jit(solution)/shard_map/all_gather | solution.py:321
  8.0 235.3 %all-gather.13.cloned.1.call-start = ((), (), s32[]{:S(2)}) async-start(), calls=%async_computation.16 | async-start | bytes 1310720 | tf_op jit(solution)/shard_map/all_gather | solution.py:322
  33.0 79.2 %collective-permute-start.1 = (f32[1,1024]{1,0:T(1,128)S(1)}, f32[1,1024]{1,0:T(1,128)S(1)}, u32[]{:S(2)}, u32[]{:S(2)}) collective-permute-start(f32[1,1024]{1,0:T(1,128)S(1)} %slice.333), channel_id=1, source_target_pairs={{0,2},{2,4},{4,6},{1,3},{3,5},{5,7},{8,10},{10,12},{12,14},{9,11},... | collective-permute-start | bytes 12296 | tf_op jit(solution)/shard_map/ppermute | solution.py:18
  37.6 72.6 %collective-permute-start = (f32[1]{0:T(128)}, f32[1]{0:T(128)}, u32[]{:S(2)}, u32[]{:S(2)}) collective-permute-start(f32[1]{0:T(128)} %get-tuple-element.1221), channel_id=1, source_target_pairs={{0,2},{2,4},{4,6},{1,3},{3,5},{5,7},{8,10},{10,12},{12,14},{9,11},... | collective-permute-start | bytes 20 | tf_op jit(solution)/shard_map/ppermute | solution.py:18
  41.5 226.4 %all-reduce.20.cloned.1.call-start = ((), (), s32[]{:S(2)}) async-start(), calls=%async_computation.17 | async-start | bytes 524288 | tf_op jit(solution)/shard_map/psum | solution.py:424
  245.6 105.8 %all-gather.15.cloned.1.call-start = ((), (), s32[]{:S(2)}) async-start(), calls=%async_computation.18 | async-start | bytes 5242880 | tf_op jit(solution)/shard_map/all_gather | solution.py:325
  246.2 185.8 %all-gather.17.cloned.1.call-start = ((), (), s32[]{:S(2)}) async-start(), calls=%async_computation.19 | async-start | bytes 5242880 | tf_op jit(solution)/shard_map/all_gather | solution.py:326
  246.8 208.8 %all-reduce.22.cloned.1.call-start = ((), (), s32[]{:S(2)}) async-start(), calls=%async_computation.20 | async-start | bytes 524288 | tf_op jit(solution)/shard_map/psum | solution.py:442
  271.3 14.3 %collective-permute-start.2 = (f32[1,1024]{1,0:T(1,128)S(1)}, f32[1,1024]{1,0:T(1,128)S(1)}, u32[]{:S(2)}, u32[]{:S(2)}) collective-permute-start(f32[1,1024]{1,0:T(1,128)S(1)} %slice.366), channel_id=1, source_target_pairs={{0,2},{2,4},{4,6},{1,3},{3,5},{5,7},{8,10},{10,12},{12,14},{9,11},... | collective-permute-start | bytes 12296 | tf_op jit(solution)/shard_map/ppermute | solution.py:18
  438.9 334.0 %all-reduce.24.cloned.1.call-start = ((), (), s32[]{:S(2)}) async-start(), calls=%async_computation.38 | async-start | bytes 2244608 | tf_op jit(solution)/shard_map/psum | solution.py:435
  457.3 5.5 collective-permute-start.3
  504.8 217.5 %copy-start.73 = (f32[128,8]{0,1:T(8,128)S(1)}, f32[128,8]{0,1:T(8,128)}, u32[]{:S(2)}) copy-start(f32[128,8]{0,1:T(8,128)} %get-tuple-element.1153) | copy-start | bytes 12292
  504.8 217.5 %copy-start.79 = (f32[8,64]{1,0:T(8,128)S(1)}, f32[8,64]{1,0:T(8,128)}, u32[]{:S(2)}) copy-start(f32[8,64]{1,0:T(8,128)} %copy.571) | copy-start | bytes 6148
  752.8 100.4 %reduce-scatter.38.cloned.1.call-start = ((), (), s32[]{:S(2)}) async-start(), calls=%async_computation.27 | async-start | bytes 5242880 | tf_op jit(solution)/shard_map/reduce_scatter | solution.py:262
  756.2 176.8 %reduce-scatter.42.cloned.1.call-start = ((), (), s32[]{:S(2)}) async-start(), calls=%async_computation.30 | async-start | bytes 5242880 | tf_op jit(solution)/shard_map/reduce_scatter | solution.py:265
  760.5 195.5 %reduce-scatter.36.cloned.1.call-start = ((), (), s32[]{:S(2)}) async-start(), calls=%async_computation.26 | async-start | bytes 368640 | tf_op jit(solution)/shard_map/reduce_scatter | solution.py:259
  763.2 212.8 %reduce-scatter.26.cloned.1.call-start = ((), (), s32[]{:S(2)}) async-start(), calls=%async_computation.21 | async-start | bytes 40960 | tf_op jit(solution)/shard_map/reduce_scatter | solution.py:244
  781.0 5.5 collective-permute-start.4
  798.1 201.0 %reduce-scatter.34.cloned.1.call-start = ((), (), s32[]{:S(2)}) async-start(), calls=%async_computation.25 | async-start | bytes 737280 | tf_op jit(solution)/shard_map/reduce_scatter | solution.py:256
  800.1 227.4 %reduce-scatter.30.cloned.1.call-start = ((), (), s32[]{:S(2)}) async-start(), calls=%async_computation.23 | async-start | bytes 1310720 | tf_op jit(solution)/shard_map/reduce_scatter | solution.py:253
  802.6 286.1 %reduce-scatter.28.cloned.1.call-start = ((), (), s32[]{:S(2)}) async-start(), calls=%async_computation.22 | async-start | bytes 3932160 | tf_op jit(solution)/shard_map/reduce_scatter | solution.py:250
  807.9 311.3 %reduce-scatter.40.cloned.1.call-start = ((), (), s32[]{:S(2)}) async-start(), calls=%async_computation.28 | async-start | bytes 1310720 | tf_op jit(solution)/shard_map/reduce_scatter | solution.py:291
  853.3 296.6 %reduce-scatter.44.cloned.1.call-start = ((), (), s32[]{:S(2)}) async-start(), calls=%async_computation.31 | async-start | bytes 1310720 | tf_op jit(solution)/shard_map/reduce_scatter | solution.py:294
  933.0 238.5 %reduce-scatter.48.cloned.1.call-start = ((), (), s32[]{:S(2)}) async-start(), calls=%async_computation.34 | async-start | bytes 20480
  935.2 216.0 %copy-start.52 = (f32[128,8,64]{0,2,1:T(8,128)S(1)}, f32[128,8,64]{0,2,1:T(8,128)}, u32[]{:S(2)}) copy-start(f32[128,8,64]{0,2,1:T(8,128)} %get-tuple-element.1147) | copy-start | bytes 786436
  935.2 261.7 %reduce-scatter.52.cloned.1.call-start = ((), (), s32[]{:S(2)}) async-start(), calls=%async_computation.36 | async-start | bytes 163840
  957.7 266.2 %reduce-scatter.46.cloned.1.call-start = ((), (), s32[]{:S(2)}) async-start(), calls=%async_computation.33 | async-start | bytes 81920
  977.5 272.6 %reduce-scatter.54.cloned.1.call-start = ((), (), s32[]{:S(2)}) async-start(), calls=%async_computation.37 | async-start | bytes 184320
  999.1 278.2 %reduce-scatter.32.cloned.1.call-start = ((), (), s32[]{:S(2)}) async-start(), calls=%async_computation.24 | async-start | bytes 327680 | tf_op jit(solution)/shard_map/reduce_scatter | solution.py:282
  1027.6 279.3 %reduce-scatter.50.cloned.1.call-start = ((), (), s32[]{:S(2)}) async-start(), calls=%async_computation.35 | async-start | bytes 983040
  1091.3 244.1 %all-gather.19.cloned.1.call-start = ((), (), s32[]{:S(2)}) async-start(), calls=%async_computation.29 | async-start | bytes 1310720 | tf_op jit(solution)/shard_map/all_gather | solution.py:570
  1119.2 244.6 %all-gather.21.cloned.1.call-start = ((), (), s32[]{:S(2)}) async-start(), calls=%async_computation.32 | async-start | bytes 1310720 | tf_op jit(solution)/shard_map/all_gather | solution.py:573
  (111 other events, 4036.4 us)
Sparse Core Ops, SparseCore 0:
  9.6 75.2 all-gather.10
  86.4 32.5 all-gather.12
  245.7 22.1 all-reduce.19
  269.4 81.9 all-gather.14
  352.8 79.0 all-gather.16
  439.0 16.4 all-reduce.21
  752.9 19.8 all-reduce.23
  775.2 78.0 reduce-scatter.37
  855.7 77.2 reduce-scatter.41
  935.7 20.3 reduce-scatter.35
  958.9 17.1 reduce-scatter.25
  978.9 20.1 reduce-scatter.33
  1002.0 25.4 reduce-scatter.29
  1029.7 58.8 reduce-scatter.27
  1091.4 27.7 reduce-scatter.39
  1122.2 27.7 reduce-scatter.43
  1152.6 18.8 reduce-scatter.47
  1174.9 21.9 reduce-scatter.51
  1200.2 23.6 reduce-scatter.45
  1226.8 23.3 reduce-scatter.53
  1253.2 24.0 reduce-scatter.31
  1280.7 26.0 reduce-scatter.49
  1308.7 26.7 all-gather.18
  1337.2 26.6 all-gather.20
where the time goes:
time: 1390 us; the launch traced here: 1370 us
  waiting for transfers between devices  649 us (47%)
  matrix products  234 us (17%)
  blocking collectives  201 us (14%)
  local copies, waits for them, and re-layouts  165 us (12%)
  other arithmetic  85.6 us (6%)
  between operations  18.6 us (1%)
  starting transfers between devices  14.7 us (1%)
    reduce_scatter x1, waiting for transfers between devices, to_owners(): lax.psum_scatter(members[7].astype(jnp.bfloat16), 'shard', scatter_dimens...  79.6 us
    all_gather x1, waiting for transfers between devices, per_device(): lax.all_gather(channel_value_weight, 'shard', axis=1, tiled=True)  77.6 us
    unnamed x29, waiting for transfers between devices  67.9 us
    all_gather x1, waiting for transfers between devices, per_device(): lax.all_gather(channel_key_weight, 'shard', axis=0, tiled=True)  64.9 us
    reduce_scatter x1, waiting for transfers between devices, to_owners(): lax.psum_scatter(members[2].astype(jnp.bfloat16), 'shard', scatter_dimens...  61 us
    reduce_scatter x1, waiting for transfers between devices, to_owners(): lax.psum_scatter(members[6].astype(jnp.bfloat16), 'shard', scatter_dimens...  45.3 us
    dynamic_slice x96, local copies, waits for them, and re-layouts, run_local(): final, outputs = lax.scan(jax.checkpoint(block_step), start, inputs)  41.5 us
    reduce_scatter x1, waiting for transfers between devices, over_blocks(): lax.psum_scatter(members[7].astype(jnp.bfloat16), 'ctx', scatter_dimensio...  30.7 us
  transfers between devices with their start and end apart: 29, of which 24 were waited for; matrix products, arithmetic and copies ran while one was open for 14% of the time, Pallas kernels for 0%

commit v1 on v0

v1 whole, which is shorter than its diff:
```python
import functools
import math

import jax
import jax.numpy as jnp
from jax import lax
from jax.experimental import pallas as pl
from jax.experimental.pallas import tpu as pltpu
from jax.sharding import PartitionSpec as P

DECAY_LOW_RANK = 64
RATE_RANK = 64
VALUE_RANK = 32


highest = lax.Precision.HIGHEST


def passed_along(block, axis, distance):
    devices = range(lax.axis_size(axis))
    route = [(i - distance, i) for i in devices if i - distance in devices]
    return lax.ppermute(block, axis, route)


def matrix_product(left, right):
    return jnp.dot(left, right, preferred_element_type=jnp.float32)


def inner_product(left, right):
    return lax.dot_general(
        left, right, (((0,), (0,)), ((), ())), preferred_element_type=jnp.float32
    )


def across_heads(left, right):
    return lax.dot_general(
        left, right, (((1,), (1,)), ((), ())), preferred_element_type=jnp.float32
    )


def layer_norm(values, gain, bias):
    mean = jnp.mean(values, -1, keepdims=True)
    centred = values - mean
    spread = jnp.mean(centred * centred, -1, keepdims=True)
    return centred * lax.rsqrt(spread + 1e-05) * gain + bias


def token_mix(standardized_vectors, prev_row, keep, blend_amounts):
    shifted = jnp.concatenate([prev_row, standardized_vectors[:-1]], 0) * keep[:, None]
    delta = shifted - standardized_vectors
    return standardized_vectors[None] + delta[None] * blend_amounts[:, None, :]


def head_leading(
    receptance_before,
    key_before_norm,
    value_before_mix,
    decay_low_rank,
    rate_low_rank,
    value_low_rank,
    first_layer_values,
    blend_amounts,
):
    count = receptance_before.shape[0]
    heads = blend_amounts.shape[1]

    def split_parts(item_entry):
        return item_entry.reshape(count, heads, -1)

    decay_logarithm = -jax.nn.softplus(-(blend_amounts[0] + split_parts(decay_low_rank))) - 0.5
    log_decay = -jnp.exp(decay_logarithm)
    rate_values = jax.nn.sigmoid(blend_amounts[1] + split_parts(rate_low_rank))
    lookup_projected_vectors = split_parts(key_before_norm)
    content_projected_vectors = split_parts(value_before_mix)
    content_projected_vectors = content_projected_vectors + (
        split_parts(first_layer_values) - content_projected_vectors
    ) * jax.nn.sigmoid(blend_amounts[2] + split_parts(value_low_rank))
    removal = lookup_projected_vectors * blend_amounts[3]
    removal = removal * lax.rsqrt(jnp.sum(removal * removal, -1, keepdims=True) + 1e-06)
    lookup_projected_vectors = lookup_projected_vectors * (
        1.0 + (rate_values - 1.0) * blend_amounts[4]
    )
    return (
        split_parts(receptance_before),
        log_decay,
        lookup_projected_vectors,
        content_projected_vectors,
        -removal,
        removal * rate_values,
    )


def exact_dot(left, right, left_dim, right_dim):
    return lax.dot_general(
        left,
        right,
        (((left_dim,), (right_dim,)), ((), ())),
        precision=highest,
        preferred_element_type=jnp.float32,
    )


def block_masks(reset_column, reset_row):
    length = reset_column.shape[0]
    rows = lax.broadcasted_iota(jnp.int32, (length, length), 0)
    cols = lax.broadcasted_iota(jnp.int32, (length, length), 1)
    same = reset_column == reset_row
    return rows, cols, (cols < rows) & same, (cols <= rows) & same


def scaled_parts(r, k, a, b, total, log_w, first, same_last):
    length = total.shape[0]
    before = total - log_w
    centre = total[length // 2 - 1 : length // 2]
    last = total[length - 1 : length]
    grow_before = jnp.exp(before - centre)
    grow_total = jnp.exp(total - centre)
    shrink = jnp.exp(centre - total)
    start_before = jnp.exp(before) * first
    start_total = jnp.exp(total) * first
    tail = jnp.exp(last - total) * same_last
    return grow_before, grow_total, shrink, start_before, start_total, tail, jnp.exp(last)


def chain_forward_kernel(
    r_ref, w_ref, k_ref, v_ref, a_ref, b_ref, col_ref, row_ref,
    raw_trans_ref, raw_off_ref, state_ref, inverse_ref, pull_state_ref, pull_own_ref,
):
    width = state_ref.shape[1]
    heads = state_ref.shape[0]
    length = r_ref.shape[0]
    col = col_ref[...]
    rows, cols, mask_before, mask_after = block_masks(col, row_ref[...])
    first = (col == 0.0).astype(jnp.float32)
    same_last = (col == col[length - 1 : length]).astype(jnp.float32)
    log_all = w_ref[...]
    total_all = exact_dot((cols <= rows).astype(jnp.float32), log_all, 1, 0)
    unit = (cols == rows).astype(jnp.float32)
    here = [slice(h * width, (h + 1) * width) for h in range(heads)]
    stage = []
    for h in range(heads):
        at = here[h]
        r, k, a, b, v = r_ref[:, at], k_ref[:, at], a_ref[:, at], b_ref[:, at], v_ref[:, at]
        gb, gt, sh, sb, st, tail, end = scaled_parts(
            r, k, a, b, total_all[:, at], log_all[:, at], first, same_last
        )
        left = jnp.concatenate([a * gb, r * gt], 0)
        right = jnp.concatenate([b * sh, k * sh], 0)
        cross = exact_dot(left, right, 1, 1)
        l_pull = jnp.where(mask_before, cross[:length, :length], 0.0)
        l_key = jnp.where(mask_before, cross[:length, length:], 0.0)
        q_pull = jnp.where(mask_after, cross[length:, :length], 0.0)
        q_key = jnp.where(mask_after, cross[length:, length:], 0.0)
        stage.append((l_pull, l_key, q_pull, q_key, a * sb, r * st, b * tail, k * tail, v, end))
    solvers = [
        unit + jnp.where(rows // 2 == cols // 2, stage[h][0], 0.0) for h in range(heads)
    ]
    size = 2
    while size < length:
        strip = (rows // (2 * size) == cols // (2 * size)) & (rows // size != cols // size)
        inner = [
            exact_dot(jnp.where(strip, stage[h][0], 0.0), solvers[h], 1, 0) for h in range(heads)
        ]
        solvers = [solvers[h] + exact_dot(solvers[h], inner[h], 1, 0) for h in range(heads)]
        size *= 2
    for h in range(heads):
        at = here[h]
        l_pull, l_key, q_pull, q_key, a0, r0, b_tail, k_tail, v, end = stage[h]
        keyed = exact_dot(l_key, v, 1, 0)
        both = exact_dot(solvers[h], jnp.concatenate([a0, keyed], 1), 1, 0)
        pull_state, pull_own = both[:, :width], both[:, width:]
        out = exact_dot(q_pull, both, 1, 0)
        raw_trans_ref[:, at] = r0 + out[:, :width]
        raw_off_ref[:, at] = out[:, width:] + exact_dot(q_key, v, 1, 0)
        final = exact_dot(both, b_tail, 0, 0)
        diagonal = jnp.where(
            lax.broadcasted_iota(jnp.int32, (width, width), 0)
            == lax.broadcasted_iota(jnp.int32, (width, width), 1),
            end * first[length - 1 : length],
            0.0,
        )
        state_ref[h, :, :width] = final[:width] + diagonal
        state_ref[h, :, width:] = final[width:] + exact_dot(v, k_tail, 0, 0)
        inverse_ref[h] = solvers[h]
        pull_state_ref[:, at] = pull_state
        pull_own_ref[:, at] = pull_own


def chain_backward_kernel(
    r_ref, w_ref, k_ref, v_ref, a_ref, b_ref, col_ref, row_ref,
    inverse_ref, pull_state_ref, pull_own_ref, start_ref, d_end_ref, d_raw_ref,
    dr_ref, dw_ref, dk_ref, dv_ref, da_ref, db_ref,
):
    width = start_ref.shape[1]
    heads = start_ref.shape[0]
    length = r_ref.shape[0]
    col = col_ref[...]
    rows, cols, mask_before, mask_after = block_masks(col, row_ref[...])
    first = (col == 0.0).astype(jnp.float32)
    same_last = (col == col[length - 1 : length]).astype(jnp.float32)
    log_all = w_ref[...]
    total_all = exact_dot((cols <= rows).astype(jnp.float32), log_all, 1, 0)
    is_last = lax.broadcasted_iota(jnp.int32, (length, width), 0) == length - 1
    reverse = (cols >= rows).astype(jnp.float32)
    for h in range(heads):
        at = slice(h * width, (h + 1) * width)
        r, k, a, b, v = r_ref[:, at], k_ref[:, at], a_ref[:, at], b_ref[:, at], v_ref[:, at]
        start, d_end, d_raw = start_ref[h], d_end_ref[h], d_raw_ref[:, at]
        gb, gt, sh, sb, st, tail, end = scaled_parts(
            r, k, a, b, total_all[:, at], log_all[:, at], first, same_last
        )
        a_s, r_s, b_s, k_s = a * gb, r * gt, b * sh, k * sh
        a0, r0, b_tail, k_tail = a * sb, r * st, b * tail, k * tail
        left = jnp.concatenate([a_s, r_s], 0)
        right = jnp.concatenate([b_s, k_s], 0)
        cross = exact_dot(left, right, 1, 1)
        l_key = jnp.where(mask_before, cross[:length, length:], 0.0)
        q_pull = jnp.where(mask_after, cross[length:, :length], 0.0)
        q_key = jnp.where(mask_after, cross[length:, length:], 0.0)
        pulled = pull_own_ref[:, at] + exact_dot(pull_state_ref[:, at], start, 1, 1)
        d_pulled = exact_dot(q_pull, d_raw, 0, 0) + exact_dot(b_tail, d_end, 1, 1)
        d_right = exact_dot(inverse_ref[h], d_pulled, 0, 0)
        dv_ref[:, at] = (
            exact_dot(q_key, d_raw, 0, 0)
            + exact_dot(k_tail, d_end, 1, 1)
            + exact_dot(l_key, d_right, 0, 0)
        )
        d_left_rows = jnp.concatenate([d_right, d_raw], 0)
        d_cross = exact_dot(d_left_rows, jnp.concatenate([pulled, v], 0), 1, 1)
        mask_left = jnp.concatenate([mask_before, mask_after], 0)
        d_cross = jnp.where(jnp.concatenate([mask_left, mask_left], 1), d_cross, 0.0)
        d_left = exact_dot(d_cross, right, 1, 0)
        d_scaled = exact_dot(d_cross, left, 0, 0)
        d_a_s, d_r_s = d_left[:length], d_left[length:]
        d_b_s, d_k_s = d_scaled[:length], d_scaled[length:]
        d_start = exact_dot(d_left_rows, start, 1, 0)
        d_a0, d_r0 = d_start[:length], d_start[length:]
        d_tail = exact_dot(jnp.concatenate([pulled, v], 0), d_end, 1, 0)
        d_b_tail, d_k_tail = d_tail[:length], d_tail[length:]
        da_ref[:, at] = d_a_s * gb + d_a0 * sb
        dr_ref[:, at] = d_r_s * gt + d_r0 * st
        db_ref[:, at] = d_b_s * sh + d_b_tail * tail
        dk_ref[:, at] = d_k_s * sh + d_k_tail * tail
        tails = d_b_tail * b_tail + d_k_tail * k_tail
        d_before = d_a_s * a_s + d_a0 * a0
        d_total = d_before + d_r_s * r_s + d_r0 * r0 - d_b_s * b_s - d_k_s * k_s - tails
        d_last = (
            jnp.sum(tails, 0, keepdims=True)
            + jnp.sum(start * d_end, 0, keepdims=True) * end * first[length - 1 : length]
        )
        d_total = d_total + jnp.where(is_last, d_last, 0.0)
        dw_ref[:, at] = exact_dot(reverse, d_total, 1, 0) - d_before


def chain_specs(length, heads, width, group):
    wide = pl.BlockSpec((length, group * width), lambda i: (0, i))
    col = pl.BlockSpec((length, 1), lambda i: (0, 0))
    row = pl.BlockSpec((1, length), lambda i: (0, 0))
    square = pl.BlockSpec((group, length, length), lambda i: (i, 0, 0))
    state = pl.BlockSpec((group, width, width), lambda i: (i, 0, 0))
    state2 = pl.BlockSpec((group, width, 2 * width), lambda i: (i, 0, 0))
    return wide, col, row, square, state, state2


def run_chain(rows, resets, heads, width):
    length = resets.shape[0]
    group = math.gcd(heads, 4)
    wide, col, row, square, state, state2 = chain_specs(length, heads, width, group)
    f32 = jnp.float32
    flat = jax.ShapeDtypeStruct((length, heads * width), f32)
    return pl.pallas_call(
        chain_forward_kernel,
        grid=(heads // group,),
        in_specs=[wide] * 6 + [col, row],
        out_specs=[wide, wide, state2, square, wide, wide],
        out_shape=[
            flat,
            flat,
            jax.ShapeDtypeStruct((heads, width, 2 * width), f32),
            jax.ShapeDtypeStruct((heads, length, length), f32),
            flat,
            flat,
        ],
        compiler_params=pltpu.CompilerParams(vmem_limit_bytes=40 * 1024 * 1024),
        cost_estimate=pl.CostEstimate(
            flops=heads * 20 * 2 * length**3 * 6, bytes_accessed=4 * 1024 * 1024, transcendentals=0
        ),
    )(*rows, resets[:, None], resets[None, :])


def run_chain_back(rows, resets, saved, start, d_end, d_raw):
    length = resets.shape[0]
    heads, width = start.shape[0], start.shape[1]
    group = math.gcd(heads, 4)
    wide, col, row, square, state, state2 = chain_specs(length, heads, width, group)
    flat = jax.ShapeDtypeStruct((length, heads * width), jnp.float32)
    return pl.pallas_call(
        chain_backward_kernel,
        grid=(heads // group,),
        in_specs=[wide] * 6 + [col, row, square, wide, wide, state, state, wide],
        out_specs=[wide] * 6,
        out_shape=[flat] * 6,
        compiler_params=pltpu.CompilerParams(vmem_limit_bytes=40 * 1024 * 1024),
        cost_estimate=pl.CostEstimate(
            flops=heads * 20 * 2 * length**3 * 6, bytes_accessed=6 * 1024 * 1024, transcendentals=0
        ),
    )(*rows, resets[:, None], resets[None, :], *saved, start, d_end, d_raw)


def state_before(gathered):
    place = lax.axis_index("ctx")
    width = gathered.shape[2]
    state = jnp.zeros(gathered.shape[1:3] + (width,), jnp.float32)
    for hop in range(gathered.shape[0] - 1):
        part = gathered[hop]
        new = (
            jnp.einsum("hij,hjk->hik", state, part[..., :width], precision=highest)
            + part[..., width:]
        )
        state = jnp.where(hop < place, new, state)
    return state


def state_gradient_after(gathered, local):
    place = lax.axis_index("ctx")
    width = gathered.shape[2]
    state = jnp.zeros(gathered.shape[1:3] + (width,), jnp.float32)
    for hop in range(gathered.shape[0] - 1, 0, -1):
        new = (
            jnp.einsum("hij,hkj->hik", state, gathered[hop][..., :width], precision=highest)
            + local[hop].astype(jnp.float32)
        )
        state = jnp.where(hop > place, new, state)
    return state


def head_trailing(
    raw_output,
    acceptance_vectors,
    lookup_projected_vectors,
    content_projected_vectors,
    gate,
    blend_amounts,
):
    mean = jnp.mean(raw_output, -1, keepdims=True)
    centred = raw_output - mean
    spread = jnp.mean(centred * centred, -1, keepdims=True)
    standardized_vectors = (
        centred * lax.rsqrt(spread + 0.00064) * blend_amounts[6] + blend_amounts[7]
    )
    current_step_extra = (
        jnp.sum(acceptance_vectors * lookup_projected_vectors * blend_amounts[5], -1, keepdims=True)
        * content_projected_vectors
    )
    combined_result = standardized_vectors + current_step_extra
    return combined_result.reshape(gate.shape) * gate


def row_tile(height, width):
    for tile in (256, 128, 64, 32):
        if height % tile == 0 and tile * width <= 32768:
            return tile
    return 16


def reduce_kernel(count, owners, blocks, *refs):
    parts, outs = refs[:count], refs[count : 2 * count]
    landed, mine, arrived = (refs[(2 + k) * count : (3 + k) * count] for k in range(3))
    own_sem, s1, r1, s2, r2, s3, r3 = refs[5 * count :]
    place, owner = lax.axis_index("ctx"), lax.axis_index("shard")
    mesh_id = pl.DeviceIdType.MESH

    def peer(index, step, size):
        return lax.rem(index + step, size)

    barrier = pltpu.get_barrier_semaphore()
    for d in range(1, blocks):
        pl.semaphore_signal(
            barrier, inc=1, device_id={"ctx": peer(place, d, blocks)}, device_id_type=mesh_id
        )
    for d in range(1, owners):
        pl.semaphore_signal(
            barrier, inc=1, device_id={"shard": peer(owner, d, owners)}, device_id_type=mesh_id
        )
    pl.semaphore_wait(barrier, blocks + owners - 2)

    first, second, third, local = {}, {}, {}, []
    for p in range(count):
        local.append(pltpu.make_async_copy(parts[p].at[:, place], mine[p], own_sem.at[p]))
        local[p].start()
        for d in range(1, blocks):
            to = peer(place, d, blocks)
            first[p, d] = pltpu.make_async_remote_copy(
                src_ref=parts[p].at[:, to],
                dst_ref=landed[p].at[d - 1],
                send_sem=s1.at[p, d - 1],
                recv_sem=r1.at[p, d - 1],
                device_id={"ctx": to},
                device_id_type=mesh_id,
            )
            first[p, d].start()

    def finish(p):
        for d in range(1, owners):
            second[p, d].wait_recv()
        height, width = mine[p].shape[1:]
        tile = row_tile(height, width)

        @pl.loop(0, height // tile)
        def _(t):
            at = pl.ds(pl.multiple_of(t * tile, tile), tile)
            total = mine[p][owner, at, :].astype(jnp.float32)
            for d in range(owners - 1):
                total = total + arrived[p][d, at, :].astype(jnp.float32)
            outs[p][place, at, :] = total.astype(jnp.bfloat16)

        for d in range(1, blocks):
            third[p, d] = pltpu.make_async_remote_copy(
                src_ref=outs[p].at[place],
                dst_ref=outs[p].at[place],
                send_sem=s3.at[p, d - 1],
                recv_sem=r3.at[p, d - 1],
                device_id={"ctx": peer(place, d, blocks)},
                device_id_type=mesh_id,
            )
            third[p, d].start()

    for p in range(count):
        local[p].wait()
        for d in range(1, blocks):
            first[p, d].wait_recv()
        height, width = mine[p].shape[1:]
        tile = row_tile(height, width)
        steps = height // tile

        @pl.loop(0, owners)
        def _(s):
            @pl.loop(0, steps)
            def _(t):
                at = pl.ds(pl.multiple_of(t * tile, tile), tile)
                total = mine[p][s, at, :].astype(jnp.float32)
                for d in range(blocks - 1):
                    total = total + landed[p][d, s, at, :].astype(jnp.float32)
                mine[p][s, at, :] = total.astype(jnp.bfloat16)

        for d in range(1, owners):
            to = peer(owner, d, owners)
            second[p, d] = pltpu.make_async_remote_copy(
                src_ref=mine[p].at[to],
                dst_ref=arrived[p].at[d - 1],
                send_sem=s2.at[p, d - 1],
                recv_sem=r2.at[p, d - 1],
                device_id={"shard": to},
                device_id_type=mesh_id,
            )
            second[p, d].start()
        if p > 0:
            finish(p - 1)
    finish(count - 1)
    for p in range(count):
        for d in range(1, blocks):
            third[p, d].wait_recv()
    for copies in (first, second, third):
        for copy in copies.values():
            copy.wait_send()


def reduce_parts(parts):
    owners, blocks = lax.axis_size("shard"), lax.axis_size("ctx")
    count = len(parts)
    bf16 = jnp.bfloat16
    shapes = [part.shape[2:] for part in parts]
    dma = pltpu.SemaphoreType.DMA
    return pl.pallas_call(
        functools.partial(reduce_kernel, count, owners, blocks),
        in_specs=[pl.BlockSpec(memory_space=pl.ANY)] * count,
        out_specs=[pl.BlockSpec(memory_space=pltpu.VMEM)] * count,
        out_shape=[jax.ShapeDtypeStruct((blocks,) + shape, bf16) for shape in shapes],
        scratch_shapes=[pltpu.VMEM((blocks - 1, owners) + shape, bf16) for shape in shapes]
        + [pltpu.VMEM((owners,) + shape, bf16) for shape in shapes]
        + [pltpu.VMEM((owners - 1,) + shape, bf16) for shape in shapes]
        + [
            dma((count,)),
            dma((count, blocks - 1)),
            dma((count, blocks - 1)),
            dma((count, owners - 1)),
            dma((count, owners - 1)),
            dma((count, blocks - 1)),
            dma((count, blocks - 1)),
        ],
        compiler_params=pltpu.CompilerParams(
            collective_id=3, has_side_effects=True, vmem_limit_bytes=48 * 1024 * 1024
        ),
    )(*parts)


def sum_gradients(members):
    owners, blocks = lax.axis_size("shard"), lax.axis_size("ctx")
    views, flat, loose = [], [], []
    for index, member in enumerate(members):
        _, height, width = member.shape
        member = member.astype(jnp.bfloat16)
        if height % (16 * blocks) == 0 and width % 128 == 0:
            views.append((index, member.reshape(owners, blocks, height // blocks, width)))
        else:
            loose.append(index)
            flat.append(member.reshape(owners, -1))
    sizes = [part.shape[1] for part in flat]
    joined = jnp.concatenate(flat, 1)
    unit = blocks * 128 * 32
    joined = jnp.pad(joined, ((0, 0), (0, -joined.shape[1] % unit)))
    joined = joined.reshape(owners, blocks, -1, 128)
    summed = reduce_parts([view for _, view in views] + [joined])
    result = {}
    for (index, view), total in zip(views, summed):
        result[index] = total.reshape(members[index].shape[1:]).astype(jnp.float32)
    rest = summed[-1].reshape(-1).astype(jnp.float32)
    begin = 0
    for index, size in zip(loose, sizes):
        result[index] = rest[begin : begin + size].reshape(members[index].shape[1:])
        begin += size
    return [result[index] for index in range(len(members))]


def per_device(
    layer_entry_input,
    first_layer_values,
    segments,
    cotangent,
    layernorm_gain,
    layernorm_bias,
    token_shift_coefs,
    channel_coefficients,
    receptance_key_value_weight,
    output_weight,
    low_rank_down,
    low_rank_upper,
    channel_key_weight,
    channel_value_weight,
):
    gains, biases, mixes, blend_amounts, proj, out_proj, down, upper_factor, ffn_in, ffn_out = (
        lax.all_gather(layernorm_gain, "shard", axis=1, tiled=True),
        lax.all_gather(layernorm_bias, "shard", axis=1, tiled=True),
        lax.all_gather(token_shift_coefs, "shard", axis=1, tiled=True),
        lax.all_gather(channel_coefficients, "shard", axis=2, tiled=True),
        lax.all_gather(receptance_key_value_weight, "shard", axis=1, tiled=True),
        lax.all_gather(output_weight, "shard", axis=1, tiled=True),
        lax.all_gather(low_rank_down, "shard", axis=0, tiled=True),
        lax.all_gather(low_rank_upper, "shard", axis=0, tiled=True),
        lax.all_gather(channel_key_weight, "shard", axis=0, tiled=True),
        lax.all_gather(channel_value_weight, "shard", axis=1, tiled=True),
    )
    gains = gains.astype(jnp.float32)
    biases = biases.astype(jnp.float32)
    mixes = mixes.astype(jnp.float32)
    blend_amounts = blend_amounts.astype(jnp.float32)
    boundary_first = DECAY_LOW_RANK
    boundary_second = boundary_first + RATE_RANK
    boundary_third = boundary_second + VALUE_RANK
    inputs_f = layer_entry_input.astype(jnp.float32)
    seg_next = (segments + 1).astype(jnp.float32)
    standardized_vectors, norm1_back = jax.vjp(layer_norm, inputs_f, gains[0], biases[0])
    prev_row, prev_seg = passed_along((standardized_vectors[-1:], seg_next[-1:]), "ctx", 1)
    keep = jnp.concatenate(
        [
            (prev_seg == seg_next[:1]).astype(jnp.float32),
            (segments[1:] == segments[:-1]).astype(jnp.float32),
        ]
    )

    def mix_local(normed_in, prev_in, coef_in):
        return token_mix(normed_in, prev_in, keep, coef_in)

    mix_all, mix1_back = jax.vjp(mix_local, standardized_vectors, prev_row, mixes[:6])
    mixed = mix_all.astype(jnp.bfloat16)
    receptance_before = matrix_product(mixed[0], proj[0])
    key_before_norm = matrix_product(mixed[2], proj[1])
    value_before_mix = matrix_product(mixed[3], proj[2])
    decay_inner_rows = jnp.tanh(matrix_product(mixed[1], down[:, :boundary_first]))
    rate_inner_rows = matrix_product(mixed[4], down[:, boundary_first:boundary_second])
    value_inner_rows = matrix_product(mixed[3], down[:, boundary_second:boundary_third])
    gate_inner_rows = jax.nn.sigmoid(matrix_product(mixed[5], down[:, boundary_third:]))
    hidden_bfloat = [
        item_entry.astype(jnp.bfloat16)
        for item_entry in (decay_inner_rows, rate_inner_rows, value_inner_rows, gate_inner_rows)
    ]
    upper_factor_parts = [
        upper_factor[:boundary_first],
        upper_factor[boundary_first:boundary_second],
        upper_factor[boundary_second:boundary_third],
        upper_factor[boundary_third:],
    ]
    low_rank_maps = [
        matrix_product(hidden_bfloat[index_value], upper_factor_parts[index_value])
        for index_value in range(4)
    ]
    fronts, front_back = jax.vjp(
        head_leading,
        receptance_before,
        key_before_norm,
        value_before_mix,
        low_rank_maps[0],
        low_rank_maps[1],
        low_rank_maps[2],
        first_layer_values.astype(jnp.float32),
        blend_amounts,
    )
    acceptance_vectors, _, lookup_projected_vectors, content_projected_vectors, _, _ = fronts
    heads = blend_amounts.shape[1]
    width = blend_amounts.shape[2]
    count = acceptance_vectors.shape[0]
    rows = [item_entry.reshape(count, heads * width) for item_entry in fronts]
    resets = jnp.cumsum(1.0 - keep)
    raw_trans, raw_off, final_both, *saved = run_chain(rows, resets, heads, width)
    final_both, ffn_in, ffn_out = lax.optimization_barrier((final_both, ffn_in, ffn_out))
    finals = lax.all_gather(final_both, "ctx")
    incoming = state_before(finals)
    raw_trans = raw_trans.reshape(count, heads, width)
    raw_output = raw_off.reshape(count, heads, width) + jnp.einsum(
        "hvi,thi->thv", incoming, raw_trans, precision=highest
    )
    combined_result, trailing_backward = jax.vjp(
        head_trailing,
        raw_output,
        acceptance_vectors,
        lookup_projected_vectors,
        content_projected_vectors,
        low_rank_maps[3],
        blend_amounts,
    )
    merged_bf = combined_result.astype(jnp.bfloat16)
    attn = lax.psum(matrix_product(merged_bf, out_proj).astype(jnp.bfloat16), "tp").astype(
        jnp.float32
    )
    mid = inputs_f + attn
    normed2, norm2_back = jax.vjp(layer_norm, mid, gains[1], biases[1])
    prev2 = passed_along(normed2[-1:], "ctx", 1)
    mix2, mix2_back = jax.vjp(mix_local, normed2, prev2, mixes[6:])
    mix2_bf = mix2[0].astype(jnp.bfloat16)
    pre2 = matrix_product(mix2_bf, ffn_in)
    active = jax.nn.relu(pre2)
    hidden2_bf = (active * active).astype(jnp.bfloat16)
    ffn = lax.psum(matrix_product(hidden2_bf, ffn_out).astype(jnp.bfloat16), "tp").astype(
        jnp.float32
    )
    result = (mid + ffn).astype(jnp.bfloat16)
    owners = lax.axis_size("shard")

    def by_owner(left, right):
        split = right.reshape(right.shape[0], owners, -1)
        return jnp.stack([inner_product(left, split[:, s]) for s in range(owners)])

    g_ffn_out = by_owner(hidden2_bf, cotangent)
    d_pre2 = (across_heads(cotangent, ffn_out) * 2.0 * active).astype(jnp.bfloat16)
    g_ffn_in = inner_product(mix2_bf, d_pre2)
    d_mix2 = lax.psum(across_heads(d_pre2, ffn_in).astype(jnp.bfloat16), "tp").astype(jnp.float32)
    d_normed2, d_prev2, d_coef2 = mix2_back(d_mix2[None])
    d_row2 = passed_along(d_prev2, "ctx", -1)
    d_normed2 = d_normed2.at[-1:].add(d_row2)
    d_mid_norm, d_gain2, d_bias2 = norm2_back(d_normed2)
    d_mid = cotangent.astype(jnp.float32) + d_mid_norm
    d_attn_bf = d_mid.astype(jnp.bfloat16)
    g_out = by_owner(merged_bf, d_attn_bf)
    d_merged = across_heads(d_attn_bf, out_proj)
    d_raw, d_recept_post, d_keyed_post, d_valued_post, d_gate, d_coef_post = trailing_backward(
        d_merged
    )
    local_in = jnp.einsum("thv,thi->hvi", d_raw, raw_trans, precision=highest)
    d_outgoing = state_gradient_after(
        finals, lax.all_gather(local_in.astype(jnp.bfloat16), "ctx")
    )
    chain_grads = [
        item_entry.reshape(count, heads, width)
        for item_entry in run_chain_back(
            rows, resets, saved, incoming, d_outgoing, d_raw.reshape(count, heads * width)
        )
    ]
    front_grads = front_back(
        (
            d_recept_post + chain_grads[0],
            chain_grads[1],
            d_keyed_post + chain_grads[2],
            d_valued_post + chain_grads[3],
            chain_grads[4],
            chain_grads[5],
        )
    )
    d_rp_bf = front_grads[0].astype(jnp.bfloat16)
    d_kp_bf = front_grads[1].astype(jnp.bfloat16)
    d_vp_bf = front_grads[2].astype(jnp.bfloat16)
    low_rank_gradients = [
        front_grads[3].astype(jnp.bfloat16),
        front_grads[4].astype(jnp.bfloat16),
        front_grads[5].astype(jnp.bfloat16),
        d_gate.astype(jnp.bfloat16),
    ]
    d_first = front_grads[6]
    g_head = front_grads[7] + d_coef_post
    g_proj = [
        inner_product(mixed[0], d_rp_bf),
        inner_product(mixed[2], d_kp_bf),
        inner_product(mixed[3], d_vp_bf),
    ]
    gate_up_weight = jnp.concatenate(
        [
            inner_product(hidden_bfloat[index_value], low_rank_gradients[index_value])
            for index_value in range(4)
        ],
        0,
    )
    d_hidden_part = jnp.concatenate(
        [
            across_heads(low_rank_gradients[index_value], upper_factor_parts[index_value])
            for index_value in range(4)
        ],
        1,
    )
    d_xr, d_xk, d_xv, d_hidden = (
        lax.psum(across_heads(d_rp_bf, proj[0]).astype(jnp.bfloat16), "tp").astype(jnp.float32),
        lax.psum(across_heads(d_kp_bf, proj[1]).astype(jnp.bfloat16), "tp").astype(jnp.float32),
        lax.psum(across_heads(d_vp_bf, proj[2]).astype(jnp.bfloat16), "tp").astype(jnp.float32),
        lax.psum(d_hidden_part.astype(jnp.bfloat16), "tp").astype(jnp.float32),
    )
    d_pre_decay = (
        d_hidden[:, :boundary_first] * (1.0 - decay_inner_rows * decay_inner_rows)
    ).astype(jnp.bfloat16)
    d_pre_rate = d_hidden[:, boundary_first:boundary_second].astype(jnp.bfloat16)
    d_pre_value = d_hidden[:, boundary_second:boundary_third].astype(jnp.bfloat16)
    d_pre_gate = (d_hidden[:, boundary_third:] * gate_inner_rows * (1.0 - gate_inner_rows)).astype(
        jnp.bfloat16
    )
    g_down = jnp.concatenate(
        [
            inner_product(mixed[1], d_pre_decay),
            inner_product(mixed[4], d_pre_rate),
            inner_product(mixed[3], d_pre_value),
            inner_product(mixed[5], d_pre_gate),
        ],
        1,
    )
    d_mixes = jnp.stack(
        [
            d_xr,
            across_heads(d_pre_decay, down[:, :boundary_first]),
            d_xk,
            d_xv + across_heads(d_pre_value, down[:, boundary_second:boundary_third]),
            across_heads(d_pre_rate, down[:, boundary_first:boundary_second]),
            across_heads(d_pre_gate, down[:, boundary_third:]),
        ]
    )
    d_normed, d_prev, d_coef1 = mix1_back(d_mixes)
    d_row = passed_along(d_prev, "ctx", -1)
    d_normed = d_normed.at[-1:].add(d_row)
    d_input_norm, d_gain1, d_bias1 = norm1_back(d_normed)
    d_input = d_mid + d_input_norm
    row_grads = jnp.concatenate(
        [jnp.stack([d_gain1, d_gain2]), jnp.stack([d_bias1, d_bias2]), d_coef1, d_coef2], 0
    )

    def columns(member):
        split = member.reshape(member.shape[:-1] + (owners, -1))
        return jnp.moveaxis(split, -2, 0).reshape(owners, -1, split.shape[-1])

    def rows_of(member):
        return member.reshape(owners, -1, member.shape[-1])

    row_sums, sum_head, sum_r, sum_k, sum_v, sum_out, sum_down, sum_up, sum_in, sum_ffn_out = (
        sum_gradients(
            [
                columns(row_grads),
                columns(g_head),
                *[rows_of(member) for member in g_proj],
                g_out,
                rows_of(g_down),
                rows_of(gate_up_weight),
                rows_of(g_ffn_in),
                g_ffn_out,
            ]
        )
    )
    mix_rows = jnp.concatenate([row_sums[4:5], row_sums[6:11]], 0)
    return (
        result,
        d_input,
        d_first,
        row_sums[0:2],
        row_sums[2:4],
        mix_rows,
        row_sums[5],
        sum_head.reshape(g_head.shape[:-1] + (-1,)),
        jnp.stack([sum_r, sum_k, sum_v]),
        sum_out,
        sum_down,
        sum_up,
        sum_in,
        sum_ffn_out,
    )


def solution(mesh):
    return jax.shard_map(
        per_device,
        mesh=mesh,
        in_specs=(
            P(("shard", "ctx"), None),
            P(("shard", "ctx"), "tp"),
            P(("shard", "ctx")),
            P(("shard", "ctx"), None),
            P(None, "shard"),
            P(None, "shard"),
            P(None, "shard"),
            P(None, "tp", "shard"),
            P(None, "shard", "tp"),
            P("tp", "shard"),
            P("shard", None),
            P("shard", "tp"),
            P("shard", "tp"),
            P("tp", "shard"),
        ),
        out_specs=(
            P(("shard", "ctx"), None),
            P(("shard", "ctx"), None),
            P(("shard", "ctx"), "tp"),
            P(None, "shard"),
            P(None, "shard"),
            P(None, "shard"),
            P("shard"),
            P(None, "tp", "shard"),
            P(None, "shard", "tp"),
            P("tp", "shard"),
            P("shard", None),
            P("shard", "tp"),
            P("shard", "tp"),
            P("tp", "shard"),
        ),
        check_vma=False,
    )
```

time: 1390 us -> 732 us (0.53)
  waiting for transfers between devices: 649 us -> 191 us
  Pallas kernels: 0 us -> 223 us
  matrix products: 234 us -> 64.6 us
  blocking collectives: 201 us -> 94.7 us
  local copies, waits for them, and re-layouts: 165 us -> 64.3 us
  other arithmetic: 85.6 us -> 51.5 us
    reduce_scatter x10 -> x0, waiting for transfers between devices: 351 us -> none  [the longest x1 79.6 us: to_owners(): lax.psum_scatter(members[7].astype(jnp.bfloat16), 'shard', scatter_dimens...]
    pallas_call x0 -> x3, Pallas kernels: none -> 223 us  [the longest x1 188 us: reduce_parts(): pl.pallas_call(functools.partial(reduce_kernel, count, owners, blocks), i...]
    dot_general x542 -> x6, matrix products: 173 us -> 8.87 us  [the longest x3 4.6 us: state_gradient_after(): jnp.einsum('hij,hkj->hik', state, gathered[hop][..., :width], precision=h...]
    all_gather x10 -> x1, blocking collectives: 101 us -> 11.8 us  [per_device(): lax.all_gather(local_in.astype(jnp.bfloat16), 'ctx')]
    unnamed x29 -> x8, waiting for transfers between devices: 67.9 us -> 2.66 us
    dynamic_slice x104 -> x0, local copies, waits for them, and re-layouts: 45.6 us -> none  [the longest x96 41.5 us: run_local(): final, outputs = lax.scan(jax.checkpoint(block_step), start, inputs)]
    all_gather x1, waiting for transfers between devices: 64.9 us -> 19.5 us  [per_device(): lax.all_gather(channel_key_weight, 'shard', axis=0, tiled=True)]
    all_gather x1, waiting for transfers between devices: 0.01 us -> 23.3 us  [per_device(): lax.all_gather(output_weight, 'shard', axis=1, tiled=True)]
  transfers between devices with their start and end apart: 29 -> 13, of which waited for: 24 -> 9; matrix products, arithmetic and copies ran while one was open for 14% -> 10% of each run, Pallas kernels for 0% -> 2%
where the time goes in v1:
time: 732 us; the launch traced here: 721 us
  Pallas kernels  223 us (30%)
  waiting for transfers between devices  191 us (26%)
  blocking collectives  94.7 us (13%)
  matrix products  64.6 us (9%)
  local copies, waits for them, and re-layouts  64.3 us (9%)
  other arithmetic  51.5 us (7%)
  between operations  17.7 us (2%)
  starting transfers between devices  14.3 us (2%)
    pallas_call x1, Pallas kernels, reduce_parts(): pl.pallas_call(functools.partial(reduce_kernel, count, owners, blocks), i...  188 us
    all_gather x1, waiting for transfers between devices, per_device(): lax.all_gather(channel_value_weight, 'shard', axis=1, tiled=True)  79.9 us
    all_gather x1, waiting for transfers between devices, per_device(): lax.all_gather(output_weight, 'shard', axis=1, tiled=True)  23.3 us
    dot_general x14, matrix products, matrix_product(): return jnp.dot(left, right, preferred_element_type=jnp.float32)  23 us
    all_gather x1, waiting for transfers between devices, per_device(): finals = lax.all_gather(final_both, 'ctx')  21 us
    pallas_call x1, Pallas kernels, run_chain_back(): pl.pallas_call(chain_backward_kernel, grid=(heads // group,), in_specs=[w...  20.4 us
    all_gather x1, waiting for transfers between devices, per_device(): lax.all_gather(channel_key_weight, 'shard', axis=0, tiled=True)  19.5 us
    all_gather x1, blocking collectives, per_device(): lax.all_gather(low_rank_down, 'shard', axis=0, tiled=True)  18.5 us
  transfers between devices with their start and end apart: 13, of which 9 were waited for; matrix products, arithmetic and copies ran while one was open for 10% of the time, Pallas kernels for 2%

profile of v1, /device:TPU:0, one launch (start us, length us, event | category | flops | bytes accessed | tf_op | source)
XLA Modules:
  0.0 721.3 jit_solution(14041499239299812197)
XLA Ops:
  10.6 12.6 %all_gather.42 = bf16[2,1024]{1,0:T(2,128)(2,1)S(1)} all-gather(bf16[2,256]{1,0:T(2,128)(2,1)S(1)} %copy-done.123), channel_id=1, replica_groups=mesh['shard'=4,'ctx'=4,'tp'=2] {'shard'}, dimensions={1}, use_global_device_ids=true | all-gather | bytes 5120 | tf_op jit(solution)/shard_map/all_gather | solution.py:542
  23.2 7.6 %all_gather.43 = bf16[2,1024]{1,0:T(2,128)(2,1)S(1)} all-gather(bf16[2,256]{1,0:T(2,128)(2,1)S(1)} %copy-done.124), channel_id=1, replica_groups=mesh['shard'=4,'ctx'=4,'tp'=2] {'shard'}, dimensions={1}, use_global_device_ids=true | all-gather | bytes 5120 | tf_op jit(solution)/shard_map/all_gather | solution.py:543
  32.6 3.4 collective-permute-start
  36.6 3.9 collective-permute-start.1
  40.5 13.3 %all_gather.44 = bf16[7,1024]{1,0:T(8,128)(2,1)S(1)} all-gather(bf16[7,256]{1,0:T(8,128)(2,1)S(1)} %copy-done.120), channel_id=1, replica_groups=mesh['shard'=4,'ctx'=4,'tp'=2] {'shard'}, dimensions={1}, use_global_device_ids=true | all-gather | bytes 17920 | tf_op jit(solution)/shard_map/all_gather | solution.py:544
  53.9 14.5 %all_gather.46 = bf16[8,8,64]{1,0,2:T(8,128)(2,1)S(1)} all-gather(bf16[8,8,16]{1,0,2:T(8,128)(2,1)S(1)} %copy.270), channel_id=1, replica_groups=mesh['shard'=4,'ctx'=4,'tp'=2] {'shard'}, dimensions={2}, use_global_device_ids=true | all-gather | bytes 10240 | tf_op jit(solution)/shard_map/all_gather | solution.py:545
  72.3 16.4 %all_gather.48 = bf16[288,512]{1,0:T(8,128)(2,1)} all-gather(bf16[72,512]{1,0:T(8,128)(2,1)S(1)} %copy-done.93), channel_id=1, replica_groups=mesh['shard'=4,'ctx'=4,'tp'=2] {'shard'}, dimensions={0}, use_global_device_ids=true | all-gather | bytes 368640 | tf_op jit(solution)/shard_map/all_gather | solution.py:549
  88.7 18.5 %all_gather.47 = bf16[1024,288]{0,1:T(8,128)(2,1)S(1)} all-gather(bf16[256,288]{0,1:T(8,128)(2,1)S(1)} %copy-done.87), channel_id=1, replica_groups=mesh['shard'=4,'ctx'=4,'tp'=2] {'shard'}, dimensions={0}, use_global_device_ids=true | all-gather | bytes 737280 | tf_op jit(solution)/shard_map/all_gather | solution.py:548
  115.1 3.1 slice_bitcast_fusion.3
  124.6 2.6 multiply_reduce_fusion.12
  130.5 2.4 multiply_add_fusion.4
  133.0 14.4 %shard_map.245 = (f32[128,512]{1,0:T(8,128)S(1)}, f32[128,512]{1,0:T(8,128)S(1)}, f32[8,64,128]{2,1,0:T(8,128)}, f32[8,128,128]{2,1,0:T(8,128)S(1)}, f32[128,512]{1,0:T(8,128)S(1)}, /*index=5*/f32[128,512]{1,0:T(8,128)S(1)}) custom-call(f32[128,512]{1,0:T(8,128)S(1)} %fusion.28.r_ref, f32[128,512]{1,0:T(8,128)S(1)} %get-tuple-element.214.w_ref, ...), custom_call_target="tpu_custom_call" | custom-call | flops 4026531840 | bytes 4194304 | tf_op jit(solution)/shard_map/pallas_call | solution.py:271
  149.0 19.5 %all-gather.10.cloned.1.call-done = bf16[1024,2048]{1,0:T(8,128)(2,1)} async-done(((bf16[256,2048]{1,0:T(8,128)(2,1)}), bf16[1024,2048]{1,0:T(8,128)(2,1)}) %all-gather.10.cloned.1.call-update) | async-done | bytes 4194320 | tf_op jit(solution)/shard_map/all_gather | solution.py:550
  168.5 79.9 %all-gather.12.cloned.1.call-done = bf16[2048,1024]{1,0:T(8,128)(2,1)} async-done(((bf16[2048,256]{1,0:T(8,128)(2,1)}), bf16[2048,1024]{1,0:T(8,128)(2,1)}) %all-gather.12.cloned.1.call-update) | async-done | bytes 4194320 | tf_op jit(solution)/shard_map/all_gather | solution.py:551
  254.5 21.0 %all-gather.16.cloned.1.call-done = f32[32,64,128]{2,1,0:T(8,128)} async-done(((f32[8,64,128]{2,1,0:T(8,128)}), f32[32,64,128]{2,1,0:T(8,128)}) %all-gather.16.cloned.1.call-update) | async-done | bytes 1048592 | tf_op jit(solution)/shard_map/all_gather | solution.py:616
  283.9 23.3 %all-gather.14.cloned.1.call-done = bf16[512,1024]{1,0:T(8,128)(2,1)} async-done(((bf16[512,256]{1,0:T(8,128)(2,1)}), bf16[512,1024]{1,0:T(8,128)(2,1)}) %all-gather.14.cloned.1.call-update) | async-done | bytes 1048592 | tf_op jit(solution)/shard_map/all_gather | solution.py:547
  312.6 14.0 %all-reduce.16.cloned.1.call-done = bf16[128,1024]{1,0:T(8,128)(2,1)} async-done(((bf16[128,1024]{1,0:T(8,128)(2,1)}), bf16[128,1024]{1,0:T(8,128)(2,1)}) %all-reduce.16.cloned.1.call-update) | async-done | bytes 262160 | tf_op jit(solution)/shard_map/psum | solution.py:632
  330.5 3.6 collective-permute-start.2
  342.3 3.1 convolution_maximum_fusion
  351.7 2.4 fusion.10
  361.7 3.8 pad_maximum_fusion.refs_5_
  365.5 3.3 convolution_convert_fusion
  368.8 11.1 %all-reduce.18.cloned.1.call-done = bf16[128,1024]{1,0:T(8,128)(2,1)} async-done(((bf16[128,1024]{1,0:T(8,128)(2,1)}), bf16[128,1024]{1,0:T(8,128)(2,1)}) %all-reduce.18.cloned.1.call-update) | async-done | bytes 262160 | tf_op jit(solution)/shard_map/psum | solution.py:656
  399.8 11.8 %all-gather.1 = bf16[32,64,64]{2,1,0:T(8,128)(2,1)} all-gather(bf16[8,64,64]{2,1,0:T(8,128)(2,1)S(1)} %convolution_convert_fusion.19), channel_id=3, replica_groups=mesh['shard'=4,'ctx'=4,'tp'=2] {'ctx'}, dimensions={0}, use_global_device_ids=true | all-gather | bytes 327680 | tf_op jit(solution)/shard_map/all_gather | solution.py:670
  420.2 20.4 %shard_map.246 = (f32[128,512]{1,0:T(8,128)S(1)}, f32[128,512]{1,0:T(8,128)S(1)}, f32[128,512]{1,0:T(8,128)S(1)}, f32[128,512]{1,0:T(8,128)S(1)}, f32[128,512]{1,0:T(8,128)S(1)}, /*index=5*/f32[128,512]{1,0:T(8,128)S(1)}) custom-call(f32[128,512]{1,0:T(8,128)S(1)} %fusion.28.r_ref, f32[128,512]{1,0:T(8,128)S(1)} %copy-done.9, f32[128,512]{1,0:T(8,128)S(1)} %copy.282.k_ref, ...), custom_call_target="tpu_custom_call" | custom-call | flops 4026531840 | bytes 6291456 | tf_op jit(solution)/shard_map/pallas_call | solution.py:297
  441.5 2.9 add_convert_fusion.3
  448.9 2.7 multiply_reduce_fusion.8
  452.4 2.8 fusion.139
  464.3 2.4 convolution_convert_fusion.13
  474.0 15.2 %all-reduce.20.cloned.1.call-done = (bf16[128,1024]{1,0:T(8,128)(2,1)}, bf16[128,288]{0,1:T(8,128)(2,1)}, bf16[128,1024]{1,0:T(8,128)(2,1)}, bf16[128,1024]{1,0:T(8,128)(2,1)}, bf16[128,1024]{1,0:T(8,128)(2,1)}) async-done(((bf16[128,1024]{1,0:T(8,128)(2,1)}, bf16[128,288]{0,1:T(8,128)(2,1)}, bf16[128,1024]{1,0:T(8,128)(2,1)}, bf16[128,1024]{1,0:T(8,128)(2,1)}, bf16[128,1024]{1,0:T(8,128)(2,1)}), ...) | async-done | bytes 1122320 | tf_op jit(solution)/shard_map/psum | solution.py:643
  502.3 2.5 concatenate.78
  505.4 188.4 %shard_map.247 = (bf16[4,64,512]{2,1,0:T(8,128)(2,1)S(1)}, bf16[4,64,512]{2,1,0:T(8,128)(2,1)S(1)}, bf16[4,64,512]{2,1,0:T(8,128)(2,1)S(1)}, bf16[4,128,256]{2,1...) custom-call(bf16[4,4,64,512]{3,2,1,0:T(8,128)(2,1)S(1)} %bitcast.307, ...), custom_call_target="tpu_custom_call" | custom-call | tf_op jit(solution)/shard_map/pallas_call | solution.py:474
  (488 shorter events, 156.9 us)
Async XLA Ops:
  7.2 33.3 %copy-start.120 = (bf16[7,256]{1,0:T(8,128)(2,1)S(1)}, bf16[7,256]{1,0:T(8,128)(2,1)}, u32[]{:S(2)}) copy-start(bf16[7,256]{1,0:T(8,128)(2,1)} %param.24) | copy-start | bytes 10756
  7.2 46.5 %copy-start.111 = (bf16[8,8,16]{2,1,0:T(8,128)(2,1)S(1)}, bf16[8,8,16]{2,1,0:T(8,128)(2,1)}, u32[]{:S(2)}) copy-start(bf16[8,8,16]{2,1,0:T(8,128)(2,1)} %param.25) | copy-start | bytes 6148
  7.2 64.1 %copy-start.88 = (bf16[128,512]{1,0:T(8,128)(2,1)S(1)}, bf16[128,512]{1,0:T(8,128)(2,1)}, u32[]{:S(2)}) copy-start(bf16[128,512]{1,0:T(8,128)(2,1)} %param.19) | copy-start | bytes 393220
  7.3 65.0 %copy-start.93 = (bf16[72,512]{1,0:T(8,128)(2,1)S(1)}, bf16[72,512]{1,0:T(8,128)(2,1)}, u32[]{:S(2)}) copy-start(bf16[72,512]{1,0:T(8,128)(2,1)} %param.29) | copy-start | bytes 221188
  7.3 81.4 %copy-start.87 = (bf16[256,288]{0,1:T(8,128)(2,1)S(1)}, bf16[256,288]{0,1:T(8,128)(2,1)}, u32[]{:S(2)}) copy-start(bf16[256,288]{0,1:T(8,128)(2,1)} %param.28) | copy-start | bytes 442372
  7.3 107.9 %all-gather.8.cloned.1.call-start = ((), (), s32[]{:S(2)}) async-start(), calls=%async_computation | async-start | bytes 3932160 | tf_op jit(solution)/shard_map/all_gather | solution.py:546
  8.0 160.5 %all-gather.10.cloned.1.call-start = ((), (), s32[]{:S(2)}) async-start(), calls=%async_computation.1 | async-start | bytes 5242880 | tf_op jit(solution)/shard_map/all_gather | solution.py:550
  8.8 239.7 %all-gather.12.cloned.1.call-start = ((), (), s32[]{:S(2)}) async-start(), calls=%async_computation.2 | async-start | bytes 5242880 | tf_op jit(solution)/shard_map/all_gather | solution.py:551
  9.5 266.0 %all-gather.16.cloned.1.call-start = ((), (), s32[]{:S(2)}) async-start(), calls=%async_computation.6 | async-start | bytes 1310720 | tf_op jit(solution)/shard_map/all_gather | solution.py:616
  30.9 78.8 %copy-start.106 = (f32[128]{0:T(128)}, f32[128]{0:T(128)S(1)}, u32[]{:S(2)}) copy-start(f32[128]{0:T(128)S(1)} %broadcast_multiply_fusion.3) | copy-start | bytes 1540
  31.1 78.6 %copy-start.117 = (f32[128]{0:T(128)}, f32[128]{0:T(128)S(1)}, u32[]{:S(2)}) copy-start(f32[128]{0:T(128)S(1)} %fusion.129) | copy-start | bytes 1540
  32.6 76.5 %collective-permute-start = (f32[1,1024]{1,0:T(1,128)S(1)}, f32[1,1024]{1,0:T(1,128)S(1)}, u32[]{:S(2)}, u32[]{:S(2)}) collective-permute-start(f32[1,1024]{1,0:T(1,128)S(1)} %slice.403), channel_id=1, source_target_pairs={{0,2},{2,4},{4,6},{1,3},{3,5},{5,7},{8,10},{10,12},{12,14},{9,11},... | collective-permute-start | bytes 12296 | tf_op jit(solution)/shard_map/ppermute | solution.py:22
  36.6 70.7 %collective-permute-start.1 = (f32[1]{0:T(128)}, f32[1]{0:T(128)}, u32[]{:S(2)}, u32[]{:S(2)}) collective-permute-start(f32[1]{0:T(128)} %get-tuple-element.213), channel_id=1, source_target_pairs={{0,2},{2,4},{4,6},{1,3},{3,5},{5,7},{8,10},{10,12},{12,14},{9,11},... | collective-permute-start | bytes 20 | tf_op jit(solution)/shard_map/ppermute | solution.py:22
  53.8 56.0 %copy-start.86 = (bf16[7,1024]{1,0:T(8,128)(2,1)}, bf16[7,1024]{1,0:T(8,128)(2,1)S(1)}, u32[]{:S(2)}) copy-start(bf16[7,1024]{1,0:T(8,128)(2,1)S(1)} %all_gather.44) | copy-start | bytes 43012
  53.8 56.0 %copy-start.79 = (f32[6,1024]{1,0:T(8,128)}, f32[6,1024]{1,0:T(8,128)S(1)}, u32[]{:S(2)}) copy-start(f32[6,1024]{1,0:T(8,128)S(1)} %slice.405) | copy-start | bytes 73732
  69.2 39.4 %copy-start.81 = (f32[1,8,64]{1,0,2:T(1,128)}, f32[1,8,64]{1,0,2:T(1,128)S(1)}, u32[]{:S(2)}) copy-start(f32[1,8,64]{1,0,2:T(1,128)S(1)} %get-tuple-element.202) | copy-start | bytes 6148
  69.3 55.3 %copy-start.96 = (f32[8,64]{1,0:T(8,128)}, f32[8,64]{1,0:T(8,128)S(1)}, u32[]{:S(2)}) copy-start(f32[8,64]{1,0:T(8,128)S(1)} %copy.273) | copy-start | bytes 6148
  107.1 145.3 %copy-start.49 = (bf16[1024,288]{0,1:T(8,128)(2,1)}, bf16[1024,288]{0,1:T(8,128)(2,1)S(1)}, u32[]{:S(2)}) copy-start(bf16[1024,288]{0,1:T(8,128)(2,1)S(1)} %all_gather.47) | copy-start | bytes 1769476
  132.9 148.0 %copy-start.46 = (f32[128,8,64]{0,2,1:T(8,128)}, f32[128,8,64]{0,2,1:T(8,128)S(1)}, u32[]{:S(2)}) copy-start(f32[128,8,64]{0,2,1:T(8,128)S(1)} %get-tuple-element.174) | copy-start | bytes 786436
  149.0 132.8 %copy-start.14 = (f32[128,512]{1,0:T(8,128)}, f32[128,512]{1,0:T(8,128)S(1)}, u32[]{:S(2)}) copy-start(f32[128,512]{1,0:T(8,128)S(1)} %get-tuple-element.68.pull_own_ref) | copy-start | bytes 786436
  248.4 58.7 %all-gather.14.cloned.1.call-start = ((), (), s32[]{:S(2)}) async-start(), calls=%async_computation.3 | async-start | bytes 1310720 | tf_op jit(solution)/shard_map/all_gather | solution.py:547
  249.0 77.5 %all-reduce.16.cloned.1.call-start = ((), (), s32[]{:S(2)}) async-start(), calls=%async_computation.4 | async-start | bytes 524288 | tf_op jit(solution)/shard_map/psum | solution.py:632
  254.5 54.9 %copy-start.51 = (f32[128,512]{0,1:T(8,128)}, f32[128,512]{0,1:T(8,128)S(1)}, u32[]{:S(2)}) copy-start(f32[128,512]{0,1:T(8,128)S(1)} %copy.287) | copy-start | bytes 786436
  278.4 33.3 %copy-start.39 = (bf16[128,1024]{1,0:T(8,128)(2,1)S(1)}, bf16[128,1024]{1,0:T(8,128)(2,1)}, u32[]{:S(2)}) copy-start(bf16[128,1024]{1,0:T(8,128)(2,1)} %param.21) | copy-start | bytes 786436
  282.0 46.9 %copy-start.44 = (f32[128,512]{1,0:T(8,128)}, f32[128,512]{1,0:T(8,128)S(1)}, u32[]{:S(2)}) copy-start(f32[128,512]{1,0:T(8,128)S(1)} %copy.293) | copy-start | bytes 786436
  309.4 31.1 %copy-start.94 = (f32[128,8]{0,1:T(8,128)S(1)}, f32[128,8]{0,1:T(8,128)}, u32[]{:S(2)}) copy-start(f32[128,8]{0,1:T(8,128)} %get-tuple-element.171) | copy-start | bytes 12292
  309.4 70.4 %all-reduce.18.cloned.1.call-start = ((), (), s32[]{:S(2)}) async-start(), calls=%async_computation.5 | async-start | bytes 524288 | tf_op jit(solution)/shard_map/psum | solution.py:656
  310.2 31.9 %copy-start.98 = (f32[1,1024]{1,0:T(1,128)}, f32[1,1024]{1,0:T(1,128)S(1)}, u32[]{:S(2)}) copy-start(f32[1,1024]{1,0:T(1,128)S(1)} %slice.441) | copy-start | bytes 12292
  330.5 11.6 %collective-permute-start.2 = (f32[1,1024]{1,0:T(1,128)S(1)}, f32[1,1024]{1,0:T(1,128)S(1)}, u32[]{:S(2)}, u32[]{:S(2)}) collective-permute-start(f32[1,1024]{1,0:T(1,128)S(1)} %slice.439), channel_id=1, source_target_pairs={{0,2},{2,4},{4,6},{1,3},{3,5},{5,7},{8,10},{10,12},{12,14},{9,11},... | collective-permute-start | bytes 12296 | tf_op jit(solution)/shard_map/ppermute | solution.py:22
  361.4 127.8 %all-reduce.20.cloned.1.call-start = ((), (), s32[]{:S(2)}) async-start(), calls=%async_computation.7 | async-start | bytes 2244608 | tf_op jit(solution)/shard_map/psum | solution.py:643
  382.3 5.8 collective-permute-start.3
  495.5 5.5 collective-permute-start.4
  (110 other events, 756.8 us)
Sparse Core Ops, SparseCore 0:
  9.7 71.3 all-gather.7
  82.7 85.7 all-gather.9
  170.1 78.3 all-gather.11
  250.7 24.8 all-gather.15
  276.9 30.1 all-gather.13
  309.9 16.5 all-reduce.15
  361.5 18.2 all-reduce.17
  469.2 19.9 all-reduce.19
